TPU v7x, 32 devices: a whole 2x2x4 slice. The times are simulated.
32 devices in a mesh: shard: 2 (over y), context: 8 (over z, x), tensor: 2 (over core).
Axes of the slice: x: 2, y: 2, z: 4, core: 2. Of those that a mesh axis runs over, the one named last changes fastest.
Arguments:
- tokens: bfloat16 [2, 2048, 960], P('shard', ('context', 'tensor')), may hold values from -6 to 6
- positions: int32 [2, 2048], P('shard', ('context', 'tensor')), may hold values from 0 to 2047, as said below
- gain_one: float32 [960], replicated, may hold values from 0.5 to 1.5
- w_query: bfloat16 [960, 960], P(('context', 'tensor'), 'shard'), may hold values from -0.1875 to 0.1875
- key_weight: bfloat16 [320, 960], P(('context', 'tensor'), 'shard'), may hold values from -0.1875 to 0.1875
- value_weight: bfloat16 [320, 960], P(('context', 'tensor'), 'shard'), may hold values from -0.1875 to 0.1875
- w_out: bfloat16 [960, 960], P(('context', 'tensor'), 'shard'), may hold values from -6 to 6
- gain_two: float32 [960], replicated, may hold values from 0.5 to 1.5
- w_gate: bfloat16 [2560, 960], P(('context', 'tensor'), 'shard'), may hold values from -0.1875 to 0.1875
- w_up: bfloat16 [2560, 960], P(('context', 'tensor'), 'shard'), may hold values from -0.1875 to 0.1875
- w_down: bfloat16 [2560, 960], P(('context', 'tensor'), 'shard'), may hold values from -0.125 to 0.125
- cotangent: bfloat16 [2, 2048, 960], P('shard', ('context', 'tensor')), may hold values from -6 to 6
Outputs:
- output: bfloat16 [2, 2048, 960], P('shard', ('context', 'tensor'))
- grad_tokens: bfloat16 [2, 2048, 960], P('shard', ('context', 'tensor'))
- grad_gain_one: float32 [960], replicated
- grad_w_query: float32 [960, 960], P(('context', 'tensor'), 'shard')
- grad_w_key: float32 [320, 960], P(('context', 'tensor'), 'shard')
- grad_w_value: float32 [320, 960], P(('context', 'tensor'), 'shard')
- grad_w_out: float32 [960, 960], P(('context', 'tensor'), 'shard')
- grad_gain_two: float32 [960], replicated
- grad_w_gate: float32 [2560, 960], P(('context', 'tensor'), 'shard')
- grad_w_up: float32 [2560, 960], P(('context', 'tensor'), 'shard')
- grad_w_down: float32 [2560, 960], P(('context', 'tensor'), 'shard')
Inputs may be any that keep to these rules, and one draw needn't show every extreme that they name: In each sequence the positions are a permutation of 0 to 2047, and each aligned block of 128 rows (the rows of one device) holds consecutive increasing positions.
All inputs are finite; a program needn't handle non-finite values.
Results may differ from a plain program's by a relative error of at most 0.024.
Values may be sent and summed in bfloat16 or wider, within the bound.
A program may use at most 128 MiB of HBM per device.

v0:
```python
import jax
import jax.numpy as jnp
from jax import lax
from jax.sharding import PartitionSpec as P

QUERY_HEAD_COUNT = 15
KEY_VALUE_HEADS = 5
HEAD_WIDTH = 64


epsilon = 1e-05


def rms_scale(value_matrix, gain):
    return (
        value_matrix
        * lax.rsqrt(jnp.mean(value_matrix * value_matrix, axis=-1, keepdims=True) + epsilon)
        * gain
    )


def apply_rotation(value_matrix, slot_positions, heads, direction):
    head_size = value_matrix.shape[1] // heads
    half_dim = head_size // 2
    freqs = 10000.0 ** (-jnp.arange(half_dim, dtype=jnp.float32) / half_dim)
    angles = slot_positions.astype(jnp.float32)[:, None] * freqs[None, :]
    cosine = jnp.cos(angles)[:, None, :]
    sine = direction * jnp.sin(angles)[:, None, :]
    split_heads = value_matrix.reshape(value_matrix.shape[0], heads, head_size)
    first_half = split_heads[..., :half_dim]
    second_half = split_heads[..., half_dim:]
    turned = jnp.concatenate(
        [first_half * cosine - second_half * sine, second_half * cosine + first_half * sine],
        axis=-1,
    )
    return turned.reshape(value_matrix.shape)


def gather_weights(w_query, key_weight, value_weight, w_out, w_gate, w_up, w_down):
    query_w, key_w, value_w, out_w, gate_w, up_w, down_w = (
        lax.all_gather(w_query, "shard", axis=1, tiled=True),
        lax.all_gather(key_weight, "shard", axis=1, tiled=True),
        lax.all_gather(value_weight, "shard", axis=1, tiled=True),
        lax.all_gather(w_out, "shard", axis=1, tiled=True),
        lax.all_gather(w_gate, "shard", axis=1, tiled=True),
        lax.all_gather(w_up, "shard", axis=1, tiled=True),
        lax.all_gather(w_down, "shard", axis=1, tiled=True),
    )
    query_w, key_w, value_w, out_w = (
        lax.all_gather(query_w, ("context", "tensor"), axis=0, tiled=True),
        lax.all_gather(key_w, ("context", "tensor"), axis=0, tiled=True),
        lax.all_gather(value_w, ("context", "tensor"), axis=0, tiled=True),
        lax.all_gather(out_w, ("context", "tensor"), axis=0, tiled=True),
    )
    gate_w, up_w, down_w = (
        lax.all_gather(gate_w, "context", axis=0, tiled=True),
        lax.all_gather(up_w, "context", axis=0, tiled=True),
        lax.all_gather(down_w, "context", axis=0, tiled=True),
    )
    return (query_w, key_w, value_w, out_w, gate_w, up_w, down_w)


def gather_keys(rotated_keys, value_matrix):
    return (
        lax.all_gather(rotated_keys, ("context", "tensor"), axis=0, tiled=True),
        lax.all_gather(value_matrix, ("context", "tensor"), axis=0, tiled=True),
    )


def split_blocks(rows_of_keys, rows_of_values, key_places):
    grand_total = rows_of_keys.shape[0]
    rows_by_width = 512
    item_count = grand_total // rows_by_width
    return (
        rows_of_keys.reshape(item_count, rows_by_width, KEY_VALUE_HEADS, HEAD_WIDTH),
        rows_of_values.reshape(item_count, rows_by_width, KEY_VALUE_HEADS, HEAD_WIDTH),
        key_places.reshape(item_count, rows_by_width),
    )


def block_scores(heads_of_queries, key_block, query_places, place_block, score_scale):
    scores = (
        jnp.einsum(
            "ikgd,jkd->kgij", heads_of_queries, key_block, preferred_element_type=jnp.float32
        )
        * score_scale
    )
    allowed = place_block[None, None, None, :] <= query_places[None, None, :, None]
    return (scores, allowed)


def log_norms(heads_of_queries, key_blocks, place_blocks, query_places, score_scale):
    initial_shape = (
        KEY_VALUE_HEADS,
        QUERY_HEAD_COUNT // KEY_VALUE_HEADS,
        heads_of_queries.shape[0],
    )
    latest = jnp.max(query_places)

    def log_advance(carried, element):
        key_block, place_block = element

        def log_compute(state):
            running, totals = state
            scores, allowed = block_scores(
                heads_of_queries, key_block, query_places, place_block, score_scale
            )
            masked = jnp.where(allowed, scores, -1e30)
            newest = jnp.maximum(running, jnp.max(masked, axis=-1))
            weights = jnp.where(allowed, jnp.exp(masked - newest[..., None]), 0.0)
            return (newest, totals * jnp.exp(running - newest) + jnp.sum(weights, axis=-1))

        needed = jnp.min(place_block) <= latest
        return (lax.cond(needed, log_compute, lambda state: state, carried), None)

    initial = (jnp.full(initial_shape, -1e30, jnp.float32), jnp.zeros(initial_shape, jnp.float32))
    (running, totals), unused = lax.scan(log_advance, initial, (key_blocks, place_blocks))
    return running + jnp.log(totals)


def mix_values(
    heads_of_queries, key_blocks, val_blocks, place_blocks, query_places, norms, score_scale
):
    latest = jnp.max(query_places)

    def mix_advance(carried, element):
        key_block, val_block, place_block = element

        def mix_compute(state):
            rounded_sum, exact_sum = state
            scores, allowed = block_scores(
                heads_of_queries, key_block, query_places, place_block, score_scale
            )
            probs = jnp.where(allowed, jnp.exp(scores - norms[..., None]), 0.0)
            probs_low = probs.astype(jnp.bfloat16)
            leftover = (probs - probs_low.astype(jnp.float32)).astype(jnp.bfloat16)
            first_term = jnp.einsum(
                "kgij,jkd->ikgd", probs_low, val_block, preferred_element_type=jnp.float32
            )
            second_term = jnp.einsum(
                "kgij,jkd->ikgd", leftover, val_block, preferred_element_type=jnp.float32
            )
            return (rounded_sum + first_term, exact_sum + first_term + second_term)

        needed = jnp.min(place_block) <= latest
        return (lax.cond(needed, mix_compute, lambda state: state, carried), None)

    initial = (
        jnp.zeros(heads_of_queries.shape, jnp.float32),
        jnp.zeros(heads_of_queries.shape, jnp.float32),
    )
    (rounded_sum, exact_sum), unused = lax.scan(
        mix_advance, initial, (key_blocks, val_blocks, place_blocks)
    )
    return (rounded_sum, exact_sum)


def attend_back(
    heads_of_queries,
    key_blocks,
    val_blocks,
    place_blocks,
    query_places,
    norms,
    row_delta,
    head_gradient,
    score_scale,
):
    latest = jnp.max(query_places)
    rows_by_width = key_blocks.shape[1]

    def attend_advance(query_gradient, element):
        key_block, val_block, place_block = element

        def attend_compute(state):
            scores, allowed = block_scores(
                heads_of_queries, key_block, query_places, place_block, score_scale
            )
            probs = jnp.where(allowed, jnp.exp(scores - norms[..., None]), 0.0)
            grad_probs = jnp.einsum(
                "ikgd,jkd->kgij", head_gradient, val_block, preferred_element_type=jnp.float32
            )
            grad_scores = (probs * (grad_probs - row_delta[..., None])).astype(jnp.bfloat16)
            new_query = (
                state
                + jnp.einsum(
                    "kgij,jkd->ikgd", grad_scores, key_block, preferred_element_type=jnp.float32
                )
                * score_scale
            )
            grad_key = (
                jnp.einsum(
                    "kgij,ikgd->jkd",
                    grad_scores,
                    heads_of_queries,
                    preferred_element_type=jnp.float32,
                )
                * score_scale
            )
            grad_value = jnp.einsum(
                "kgij,ikgd->jkd",
                probs.astype(jnp.bfloat16),
                head_gradient,
                preferred_element_type=jnp.float32,
            )
            return (new_query, (grad_key, grad_value))

        def skipped(state):
            blank_array = jnp.zeros((rows_by_width, KEY_VALUE_HEADS, HEAD_WIDTH), jnp.float32)
            return (state, (blank_array, blank_array))

        needed = jnp.min(place_block) <= latest
        return lax.cond(needed, attend_compute, skipped, query_gradient)

    initial = jnp.zeros(heads_of_queries.shape, jnp.float32)
    query_gradient, (gradient_of_keys, value_gradient) = lax.scan(
        attend_advance, initial, (key_blocks, val_blocks, place_blocks)
    )
    grand_total = gradient_of_keys.shape[0] * gradient_of_keys.shape[1]
    return (
        query_gradient,
        gradient_of_keys.reshape(grand_total, KEY_VALUE_HEADS * HEAD_WIDTH),
        value_gradient.reshape(grand_total, KEY_VALUE_HEADS * HEAD_WIDTH),
    )


def body(
    tokens,
    positions,
    gain_one,
    w_query,
    key_weight,
    value_weight,
    w_out,
    gain_two,
    w_gate,
    w_up,
    w_down,
    cotangent,
):
    inputs = tokens[0].astype(jnp.float32)
    slot_positions = positions[0]
    incoming = cotangent[0].astype(jnp.float32)
    count_of_rows = inputs.shape[0]
    group_width = QUERY_HEAD_COUNT // KEY_VALUE_HEADS
    score_scale = HEAD_WIDTH ** (-0.5)
    query_w, key_w, value_w, out_w, gate_w, up_w, down_w = gather_weights(
        w_query, key_weight, value_weight, w_out, w_gate, w_up, w_down
    )
    normed_one = rms_scale(inputs, gain_one).astype(jnp.bfloat16)
    queries = jnp.dot(normed_one, query_w.T, preferred_element_type=jnp.float32)
    key_matrix = jnp.dot(normed_one, key_w.T, preferred_element_type=jnp.float32)
    value_matrix = jnp.dot(normed_one, value_w.T, preferred_element_type=jnp.float32).astype(
        jnp.bfloat16
    )
    rotated_queries = apply_rotation(queries, slot_positions, QUERY_HEAD_COUNT, 1.0).astype(
        jnp.bfloat16
    )
    rotated_keys = apply_rotation(key_matrix, slot_positions, KEY_VALUE_HEADS, 1.0).astype(
        jnp.bfloat16
    )
    rows_of_keys, rows_of_values = gather_keys(rotated_keys, value_matrix)
    key_places = lax.all_gather(slot_positions, ("context", "tensor"), axis=0, tiled=True)
    heads_of_queries = rotated_queries.reshape(
        count_of_rows, KEY_VALUE_HEADS, group_width, HEAD_WIDTH
    )
    key_blocks, val_blocks, place_blocks = split_blocks(rows_of_keys, rows_of_values, key_places)
    norms = log_norms(heads_of_queries, key_blocks, place_blocks, slot_positions, score_scale)
    mixed, mixed_exact = mix_values(
        heads_of_queries, key_blocks, val_blocks, place_blocks, slot_positions, norms, score_scale
    )
    mixed_low = mixed.reshape(count_of_rows, QUERY_HEAD_COUNT * HEAD_WIDTH).astype(jnp.bfloat16)
    branch = jnp.dot(mixed_low, out_w.T, preferred_element_type=jnp.float32)
    middle = inputs + branch
    normed_two = rms_scale(middle, gain_two).astype(jnp.bfloat16)
    normed_all = lax.all_gather(normed_two, "tensor", axis=0, tiled=True)
    gates = jnp.dot(normed_all, gate_w.T, preferred_element_type=jnp.float32)
    lifted = jnp.dot(normed_all, up_w.T, preferred_element_type=jnp.float32)
    hidden = (jax.nn.silu(gates) * lifted).astype(jnp.bfloat16)
    unit_part = jnp.dot(hidden, down_w, preferred_element_type=jnp.float32)
    unit_out = lax.psum_scatter(
        unit_part.astype(jnp.bfloat16), "tensor", scatter_dimension=0, tiled=True
    ).astype(jnp.float32)
    output = (middle + unit_out).astype(jnp.bfloat16)[None]
    query_w, key_w, value_w, out_w, gate_w, up_w, down_w = gather_weights(
        w_query, key_weight, value_weight, w_out, w_gate, w_up, w_down
    )
    grad_out_low = incoming.astype(jnp.bfloat16)
    grad_out_all = lax.all_gather(grad_out_low, "tensor", axis=0, tiled=True)
    grad_hidden = jnp.dot(grad_out_all, down_w.T, preferred_element_type=jnp.float32)
    grad_down = jnp.dot(hidden.T, grad_out_all, preferred_element_type=jnp.float32)
    unused_unit, pull_unit = jax.vjp(
        lambda gate_in, lift_in: jax.nn.silu(gate_in) * lift_in, gates, lifted
    )
    grad_gates, grad_lifted = pull_unit(grad_hidden)
    grad_gates = grad_gates.astype(jnp.bfloat16)
    grad_lifted = grad_lifted.astype(jnp.bfloat16)
    grad_gate_w = jnp.dot(grad_gates.T, normed_all, preferred_element_type=jnp.float32)
    grad_up_w = jnp.dot(grad_lifted.T, normed_all, preferred_element_type=jnp.float32)
    grad_norm_part = jnp.dot(grad_gates, gate_w, preferred_element_type=jnp.float32) + jnp.dot(
        grad_lifted, up_w, preferred_element_type=jnp.float32
    )
    grad_normed_two = lax.psum_scatter(
        grad_norm_part.astype(jnp.bfloat16), "tensor", scatter_dimension=0, tiled=True
    ).astype(jnp.float32)
    unused_two, pull_two = jax.vjp(rms_scale, middle, gain_two)
    grad_middle_norm, grad_gain_two = pull_two(grad_normed_two)
    grad_middle = incoming + grad_middle_norm
    grad_branch = grad_middle.astype(jnp.bfloat16)
    grad_out_w = jnp.dot(grad_branch.T, mixed_low, preferred_element_type=jnp.float32)
    mixed_gradient = jnp.dot(grad_branch, out_w, preferred_element_type=jnp.float32).astype(
        jnp.bfloat16
    )
    head_gradient = mixed_gradient.reshape(count_of_rows, KEY_VALUE_HEADS, group_width, HEAD_WIDTH)
    row_delta = jnp.sum(head_gradient.astype(jnp.float32) * mixed_exact, axis=-1).transpose(1, 2, 0)
    rows_of_keys, rows_of_values = gather_keys(rotated_keys, value_matrix)
    key_blocks, val_blocks, place_blocks = split_blocks(rows_of_keys, rows_of_values, key_places)
    query_gradient, grad_key_terms, grad_value_terms = attend_back(
        heads_of_queries,
        key_blocks,
        val_blocks,
        place_blocks,
        slot_positions,
        norms,
        row_delta,
        head_gradient,
        score_scale,
    )
    summed_keys, value_sum = (
        lax.psum_scatter(
            grad_key_terms.astype(jnp.bfloat16),
            ("context", "tensor"),
            scatter_dimension=0,
            tiled=True,
        ).astype(jnp.float32),
        lax.psum_scatter(
            grad_value_terms.astype(jnp.bfloat16),
            ("context", "tensor"),
            scatter_dimension=0,
            tiled=True,
        ).astype(jnp.float32),
    )
    grad_q = apply_rotation(
        query_gradient.reshape(count_of_rows, QUERY_HEAD_COUNT * HEAD_WIDTH),
        slot_positions,
        QUERY_HEAD_COUNT,
        -1.0,
    ).astype(jnp.bfloat16)
    key_gradient = apply_rotation(summed_keys, slot_positions, KEY_VALUE_HEADS, -1.0).astype(
        jnp.bfloat16
    )
    grad_v = value_sum.astype(jnp.bfloat16)
    grad_normed_one = (
        jnp.dot(grad_q, query_w, preferred_element_type=jnp.float32)
        + jnp.dot(key_gradient, key_w, preferred_element_type=jnp.float32)
        + jnp.dot(grad_v, value_w, preferred_element_type=jnp.float32)
    )
    grad_query_w = jnp.dot(grad_q.T, normed_one, preferred_element_type=jnp.float32)
    grad_key_w = jnp.dot(key_gradient.T, normed_one, preferred_element_type=jnp.float32)
    grad_value_w = jnp.dot(grad_v.T, normed_one, preferred_element_type=jnp.float32)
    unused_one, pull_one = jax.vjp(rms_scale, inputs, gain_one)
    grad_inputs_norm, grad_gain_one = pull_one(grad_normed_one)
    grad_tokens = (grad_middle + grad_inputs_norm).astype(jnp.bfloat16)[None]
    grad_query_w, grad_key_w, grad_value_w, grad_out_w = (
        lax.psum_scatter(
            grad_query_w.astype(jnp.bfloat16),
            ("context", "tensor"),
            scatter_dimension=0,
            tiled=True,
        ).astype(jnp.float32),
        lax.psum_scatter(
            grad_key_w.astype(jnp.bfloat16), ("context", "tensor"), scatter_dimension=0, tiled=True
        ).astype(jnp.float32),
        lax.psum_scatter(
            grad_value_w.astype(jnp.bfloat16),
            ("context", "tensor"),
            scatter_dimension=0,
            tiled=True,
        ).astype(jnp.float32),
        lax.psum_scatter(
            grad_out_w.astype(jnp.bfloat16), ("context", "tensor"), scatter_dimension=0, tiled=True
        ).astype(jnp.float32),
    )
    grad_gate_w, grad_up_w, grad_down = (
        lax.psum_scatter(
            grad_gate_w.astype(jnp.bfloat16), "context", scatter_dimension=0, tiled=True
        ).astype(jnp.float32),
        lax.psum_scatter(
            grad_up_w.astype(jnp.bfloat16), "context", scatter_dimension=0, tiled=True
        ).astype(jnp.float32),
        lax.psum_scatter(
            grad_down.astype(jnp.bfloat16), "context", scatter_dimension=0, tiled=True
        ).astype(jnp.float32),
    )
    grad_query_w, grad_key_w, grad_value_w, grad_out_w, grad_gate_w, grad_up_w, grad_down = (
        lax.psum_scatter(
            grad_query_w.astype(jnp.bfloat16), "shard", scatter_dimension=1, tiled=True
        ).astype(jnp.float32),
        lax.psum_scatter(
            grad_key_w.astype(jnp.bfloat16), "shard", scatter_dimension=1, tiled=True
        ).astype(jnp.float32),
        lax.psum_scatter(
            grad_value_w.astype(jnp.bfloat16), "shard", scatter_dimension=1, tiled=True
        ).astype(jnp.float32),
        lax.psum_scatter(
            grad_out_w.astype(jnp.bfloat16), "shard", scatter_dimension=1, tiled=True
        ).astype(jnp.float32),
        lax.psum_scatter(
            grad_gate_w.astype(jnp.bfloat16), "shard", scatter_dimension=1, tiled=True
        ).astype(jnp.float32),
        lax.psum_scatter(
            grad_up_w.astype(jnp.bfloat16), "shard", scatter_dimension=1, tiled=True
        ).astype(jnp.float32),
        lax.psum_scatter(
            grad_down.astype(jnp.bfloat16), "shard", scatter_dimension=1, tiled=True
        ).astype(jnp.float32),
    )
    grad_gain_one, grad_gain_two = lax.psum(
        (grad_gain_one, grad_gain_two), ("shard", "context", "tensor")
    )
    return (
        output,
        grad_tokens,
        grad_gain_one,
        grad_query_w,
        grad_key_w,
        grad_value_w,
        grad_out_w,
        grad_gain_two,
        grad_gate_w,
        grad_up_w,
        grad_down,
    )


def solution(mesh):
    placed = (
        P("shard", ("context", "tensor"), None),
        P("shard", ("context", "tensor")),
        P(),
        P(("context", "tensor"), "shard"),
        P(("context", "tensor"), "shard"),
        P(("context", "tensor"), "shard"),
        P(("context", "tensor"), "shard"),
        P(),
        P(("context", "tensor"), "shard"),
        P(("context", "tensor"), "shard"),
        P(("context", "tensor"), "shard"),
        P("shard", ("context", "tensor"), None),
    )
    return jax.shard_map(
        body,
        mesh=mesh,
        in_specs=placed,
        out_specs=(
            P("shard", ("context", "tensor"), None),
            P("shard", ("context", "tensor"), None),
            P(),
            P(("context", "tensor"), "shard"),
            P(("context", "tensor"), "shard"),
            P(("context", "tensor"), "shard"),
            P(("context", "tensor"), "shard"),
            P(),
            P(("context", "tensor"), "shard"),
            P(("context", "tensor"), "shard"),
            P(("context", "tensor"), "shard"),
        ),
        check_vma=False,
    )
```

profile of v0, /device:TPU:0, one launch (start us, length us, event | category | flops | bytes accessed | tf_op | source)
XLA Modules:
  0.0 926.4 jit_solution(10641644346005002408)
XLA Ops:
  9.8 5.7 all-gather.2
  15.7 24.4 %all-gather.3 = bf16[16,20,960]{2,1,0:T(8,128)(2,1)S(1)} all-gather(bf16[1,20,960]{2,1,0:T(8,128)(2,1)S(1)} %bitcast.355), channel_id=1, replica_groups=mesh['shard'=2,'context'=8,'tensor'=2] {'context','tensor'}, dimensions={0}, use_global_device_ids=true | all-gather | bytes 652800 | tf_op jit(solution)/shard_map/all_gather | solution.py:51
  42.3 4.5 all-gather.6
  47.0 21.1 %all-gather.7 = bf16[16,20,960]{2,1,0:T(8,128)(2,1)S(1)} all-gather(bf16[1,20,960]{2,1,0:T(8,128)(2,1)S(1)} %bitcast.356), channel_id=1, replica_groups=mesh['shard'=2,'context'=8,'tensor'=2] {'context','tensor'}, dimensions={0}, use_global_device_ids=true | all-gather | bytes 652800 | tf_op jit(solution)/shard_map/all_gather | solution.py:52
  69.5 5.0 all-gather.4
  75.6 4.9 all-gather.8
  81.5 6.0 all-gather.10
  89.0 6.0 all-gather.11
  96.4 6.0 all-gather.12
  103.8 18.6 %all-gather = s32[1,2048]{1,0:T(1,128)S(1)} all-gather(s32[1,128]{1,0:T(1,128)S(1)} %copy-done.32), channel_id=2, replica_groups=mesh['shard'=2,'context'=8,'tensor'=2] {'context','tensor'}, dimensions={1}, use_global_device_ids=true | all-gather | bytes 8704 | tf_op jit(solution)/shard_map/all_gather | solution.py:263
  123.7 2.5 all-gather.1
  126.1 3.2 reshape.381
  129.7 3.2 reshape.382
  134.3 27.7 %all-gather.31.cloned.1.call-done = bf16[16,60,960]{2,1,0:T(8,128)(2,1)} async-done(((bf16[1,60,960]{2,1,0:T(8,128)(2,1)}), bf16[16,60,960]{2,1,0:T(8,128)(2,1)}) %all-gather.31.cloned.1.call-update) | async-done | bytes 1843216 | tf_op jit(solution)/shard_map/all_gather | solution.py:50
  162.0 4.0 dot_general.103
  166.0 2.3 fusion.96
  168.5 15.4 %while.41 = (s32[]{:T(128)}, f32[5,3,128]{2,1,0:T(4,128)S(1)}, f32[5,3,128]{2,1,0:T(4,128)S(1)}, s32[4,512]{1,0:T(4,128)S(1)}, s32[]{:T(128)}, /*index=5*/s32[1,...) while((s32[]{:T(128)}, f32[5,3,128]{2,1,0:T(4,128)S(1)}, ...), condition=%wide.region_8.9_spmd, body=%wide.region_2.8_spmd.sunk | while | flops 133763328 | bytes 8741079 | solution.py:117
  184.0 21.7 %while.42 = (s32[]{:T(128)}, f32[128,5,3,64]{0,3,2,1:T(8,128)S(1)}, f32[128,5,3,64]{0,3,2,1:T(8,128)S(1)}, s32[4,512]{1,0:T(4,128)S(1)}, s32[]{:T(128)}, /*index...) while((s32[]{:T(128)}, f32[128,5,3,64]{0,3,2,1:T(8,128)S(1)}, ...), condition=%wide.region_13.14_spmd, body=%wide.region_9.0_spmd.sunk | while | flops 388735488 | bytes 21441308 | solution.py:152
  186.0 3.5 conditional.7
  191.4 3.5 conditional.7
  196.8 3.5 conditional.7
  202.2 3.5 conditional.7
  205.9 4.1 reshape.409
  212.5 2.4 all_gather.84
  214.9 46.0 %all-gather.25.cloned.1.call-done = bf16[1280,960]{1,0:T(8,128)(2,1)} async-done(((bf16[160,960]{1,0:T(8,128)(2,1)}), bf16[1280,960]{1,0:T(8,128)(2,1)}) %all-gather.25.cloned.1.call-update) | async-done | bytes 2457616 | tf_op jit(solution)/shard_map/all_gather | solution.py:56
  260.9 3.7 fusion.117
  264.6 52.2 %all-gather.27.cloned.1.call-done = bf16[1280,960]{1,0:T(8,128)(2,1)} async-done(((bf16[160,960]{1,0:T(8,128)(2,1)}), bf16[1280,960]{1,0:T(8,128)(2,1)}) %all-gather.27.cloned.1.call-update) | async-done | bytes 2457616 | tf_op jit(solution)/shard_map/all_gather | solution.py:57
  316.8 3.7 fusion.118
  320.5 52.3 %all-gather.29.cloned.1.call-done = bf16[1280,960]{1,0:T(8,128)(2,1)} async-done(((bf16[160,960]{1,0:T(8,128)(2,1)}), bf16[1280,960]{1,0:T(8,128)(2,1)}) %all-gather.29.cloned.1.call-update) | async-done | bytes 2457616 | tf_op jit(solution)/shard_map/all_gather | solution.py:58
  372.8 4.9 multiply_convert_fusion
  382.2 3.0 convolution_convert_fusion.7
  392.8 7.5 reduce-scatter.51.cloned.1.call-done
  404.9 36.0 %while.43 = (s32[]{:T(128)}, f32[128,5,3,64]{0,3,2,1:T(8,128)S(1)}, bf16[4,512,5,64]{1,3,2,0:T(8,128)(2,1)}, bf16[4,512,5,64]{1,3,2,0:T(8,128)(2,1)}, s32[4,512]...) while((s32[]{:T(128)}, f32[128,5,3,64]{0,3,2,1:T(8,128)S(1)}, ...), condition=%wide.region_23.24_spmd, body=%wide.region_19.23_spmd.sunk | while | flops 639615488 | bytes 23820584 | solution.py:216
  407.5 5.4 conditional.8
  408.5 2.3 fusion.40
  416.5 5.4 conditional.8
  417.5 2.3 fusion.40
  425.5 5.4 conditional.8
  426.5 2.3 fusion.40
  434.5 5.4 conditional.8
  435.5 2.3 fusion.40
  444.7 2.6 copy.84
  447.3 2.3 copy.67
  451.1 2.6 copy.86
  453.8 2.5 convolution_convert_fusion.2
  457.4 2.4 convolution_convert_fusion.1
  461.0 2.4 convolution_convert_fusion
  468.3 39.8 %reduce-scatter.55.cloned.1.call-done = bf16[128,320]{1,0:T(8,128)(2,1)} async-done(((bf16[2048,320]{1,0:T(8,128)(2,1)}), bf16[128,320]{1,0:T(8,128)(2,1)}) %reduce-scatter.55.cloned.1.call-update) | async-done | bytes 81936
  509.6 61.0 %reduce-scatter.57.cloned.1.call-done = bf16[128,320]{1,0:T(8,128)(2,1)} async-done(((bf16[2048,320]{1,0:T(8,128)(2,1)}), bf16[128,320]{1,0:T(8,128)(2,1)}) %reduce-scatter.57.cloned.1.call-update) | async-done | bytes 81936
  572.0 76.1 %fusion.112 = (bf16[64,960]{1,0:T(8,128)(2,1)S(1)}, bf16[24,960]{1,0:T(8,128)(2,1)S(1)}, bf16[24,960]{1,0:T(8,128)(2,1)S(1)}, bf16[64,960]{1,0:T(8,128)(2,1)S(1)}) fusion(bf16[960,960]{1,0:T(8,128)(2,1)} %convolution_convert_fusion.4, bf16[320,960]{1,0:T(8,128)(2,1)S(1)} %convolution_convert_fusion.6, bf16[320,960]{1,0:T(8,128)(2,1)S(1)} %convolution_convert_fusion.5, ...), kind=kCustom, calls=%all-reduce-scatter.4 | all-reduce-scatter fusion | flops 2703362 | bytes 5253632
  648.1 9.0 collective-permute-start.1
  657.1 4.2 collective-permute-start.2
  661.3 3.2 collective-permute-start.3
  665.9 2.9 collective-permute-start.5
  673.4 3.2 collective-permute-start.7
  684.2 55.6 %reduce-scatter.47.cloned.1.call-done = bf16[160,960]{1,0:T(8,128)(2,1)} async-done(((bf16[1280,960]{1,0:T(8,128)(2,1)}), bf16[160,960]{1,0:T(8,128)(2,1)}) %reduce-scatter.47.cloned.1.call-update) | async-done | bytes 307216 | tf_op jit(solution)/shard_map/reduce_scatter | solution.py:388
  742.2 4.0 reshape.401
  747.1 65.2 %reduce-scatter.49.cloned.1.call-done = bf16[160,960]{1,0:T(8,128)(2,1)} async-done(((bf16[1280,960]{1,0:T(8,128)(2,1)}), bf16[160,960]{1,0:T(8,128)(2,1)}) %reduce-scatter.49.cloned.1.call-update) | async-done | bytes 307216 | tf_op jit(solution)/shard_map/reduce_scatter | solution.py:391
  814.4 2.5 fusion.81
  816.9 39.6 %all-reduce.8 = (f32[960]{0:T(1024)}, f32[960]{0:T(1024)}) all-reduce(f32[960]{0:T(1024)S(1)} %get-tuple-element.484, f32[960]{0:T(1024)S(1)} %copy-done.41), channel_id=1, replica_groups=mesh['shard'=2,'context'=8,'tensor'=2] {'shard','context','tensor'}, use_global_device_ids=true, to_apply=%region_28.29 | all-reduce | flops 1920 | bytes 15360 | tf_op jit(solution)/shard_map/psum | solution.py:418
  862.4 5.8 reduce-scatter.65.cloned.1.call-done
  869.8 14.8 %reduce-scatter.67.cloned.1.call-done = bf16[480,160]{1,0:T(8,128)(2,1)} async-done(((bf16[960,160]{1,0:T(8,128)(2,1)}), bf16[480,160]{1,0:T(8,128)(2,1)}) %reduce-scatter.67.cloned.1.call-update) | async-done | bytes 153616
  886.5 14.5 %reduce-scatter.69.cloned.1.call-done = bf16[480,160]{1,0:T(8,128)(2,1)} async-done(((bf16[960,160]{1,0:T(8,128)(2,1)}), bf16[480,160]{1,0:T(8,128)(2,1)}) %reduce-scatter.69.cloned.1.call-update) | async-done | bytes 153616
  902.8 14.7 %reduce-scatter.71.cloned.1.call-done = bf16[480,160]{1,0:T(8,128)(2,1)} async-done(((bf16[960,160]{1,0:T(8,128)(2,1)}), bf16[480,160]{1,0:T(8,128)(2,1)}) %reduce-scatter.71.cloned.1.call-update) | async-done | bytes 153616
  (352 shorter events, 136.3 us)
Async XLA Ops:
  7.2 33.9 %copy-start = (bf16[1,128,960]{1,2,0:T(8,128)(2,1)S(1)}, bf16[1,128,960]{1,2,0:T(8,128)(2,1)}, u32[]{:S(2)}) copy-start(bf16[1,128,960]{1,2,0:T(8,128)(2,1)} %param.24) | copy-start | bytes 737284
  7.2 33.9 %copy-start.26 = (f32[960]{0:T(1024)S(1)}, f32[960]{0:T(1024)}, u32[]{:S(2)}) copy-start(f32[960]{0:T(1024)} %param.26) | copy-start | bytes 11524
  7.2 118.9 %all-gather.21.cloned.1.call-start = ((), (), s32[]{:S(2)}) async-start(), calls=%async_computation.14 | async-start | bytes 1392640 | tf_op jit(solution)/shard_map/all_gather | solution.py:65
  8.4 157.6 %copy-start.38 = (f32[128]{0:T(128)}, f32[128]{0:T(128)S(1)}, u32[]{:S(2)}) copy-start(f32[128]{0:T(128)S(1)} %fusion.106) | copy-start | bytes 1540
  15.6 26.7 %copy-start.40 = (bf16[20,480]{1,0:T(8,128)(2,1)S(1)}, bf16[20,480]{1,0:T(8,128)(2,1)}, u32[]{:S(2)}) copy-start(bf16[20,480]{1,0:T(8,128)(2,1)} %param.29) | copy-start | bytes 57604
  40.0 28.0 %copy-start.6 = (bf16[16,20,960]{2,1,0:T(8,128)(2,1)}, bf16[16,20,960]{2,1,0:T(8,128)(2,1)S(1)}, u32[]{:S(2)}) copy-start(bf16[16,20,960]{2,1,0:T(8,128)(2,1)S(1)} %all-gather.3) | copy-start | bytes 1843204
  41.6 28.0 %copy-start.35 = (bf16[60,480]{1,0:T(8,128)(2,1)S(1)}, bf16[60,480]{1,0:T(8,128)(2,1)}, u32[]{:S(2)}) copy-start(bf16[60,480]{1,0:T(8,128)(2,1)} %param.27) | copy-start | bytes 172804
  42.3 87.4 %all-gather.23.cloned.1.call-start = ((), (), s32[]{:S(2)}) async-start(), calls=%async_computation.15 | async-start | bytes 1392640 | tf_op jit(solution)/shard_map/all_gather | solution.py:66
  47.0 28.6 %copy-start.36 = (bf16[60,480]{1,0:T(8,128)(2,1)S(1)}, bf16[60,480]{1,0:T(8,128)(2,1)}, u32[]{:S(2)}) copy-start(bf16[60,480]{1,0:T(8,128)(2,1)} %param.30) | copy-start | bytes 172804
  68.1 13.5 %copy-start.28 = (bf16[160,480]{1,0:T(8,128)(2,1)S(1)}, bf16[160,480]{1,0:T(8,128)(2,1)}, u32[]{:S(2)}) copy-start(bf16[160,480]{1,0:T(8,128)(2,1)} %param.32) | copy-start | bytes 460804
  68.4 19.5 %copy-start.11 = (bf16[320,960]{1,0:T(8,128)(2,1)}, bf16[320,960]{1,0:T(8,128)(2,1)S(1)}, u32[]{:S(2)}) copy-start(bf16[320,960]{1,0:T(8,128)(2,1)S(1)} %reshape.405) | copy-start | bytes 1843204
  69.5 19.5 %copy-start.29 = (bf16[160,480]{1,0:T(8,128)(2,1)S(1)}, bf16[160,480]{1,0:T(8,128)(2,1)}, u32[]{:S(2)}) copy-start(bf16[160,480]{1,0:T(8,128)(2,1)} %param.33) | copy-start | bytes 460804
  69.5 92.6 %all-gather.31.cloned.1.call-start = ((), (), s32[]{:S(2)}) async-start(), calls=%async_computation.22 | async-start | bytes 2228224 | tf_op jit(solution)/shard_map/all_gather | solution.py:50
  75.5 130.3 %all-gather.33.cloned.1.call-start = ((), (), s32[]{:S(2)}) async-start(), calls=%async_computation.23 | async-start | bytes 2228224 | tf_op jit(solution)/shard_map/all_gather | solution.py:53
  81.5 179.4 %all-gather.25.cloned.1.call-start = ((), (), s32[]{:S(2)}) async-start(), calls=%async_computation.16 | async-start | bytes 2949120 | tf_op jit(solution)/shard_map/all_gather | solution.py:56
  87.5 8.9 copy-start.30
  88.9 227.9 %all-gather.27.cloned.1.call-start = ((), (), s32[]{:S(2)}) async-start(), calls=%async_computation.17 | async-start | bytes 2949120 | tf_op jit(solution)/shard_map/all_gather | solution.py:57
  95.0 8.8 copy-start.32
  95.0 28.7 %copy-start.21 = (bf16[1,128,960]{1,2,0:T(8,128)(2,1)S(1)}, bf16[1,128,960]{1,2,0:T(8,128)(2,1)}, u32[]{:S(2)}) copy-start(bf16[1,128,960]{1,2,0:T(8,128)(2,1)} %param.35) | copy-start | bytes 737284
  96.3 276.5 %all-gather.29.cloned.1.call-start = ((), (), s32[]{:S(2)}) async-start(), calls=%async_computation.18 | async-start | bytes 2949120 | tf_op jit(solution)/shard_map/all_gather | solution.py:58
  103.7 285.1 %reduce-scatter.53.cloned.1.call-start = ((), (), s32[]{:S(2)}) async-start(), calls=%async_computation.25 | async-start | bytes 786432
  205.7 4.2 copy-start.19
  205.8 4.2 copy-start.27
  205.8 4.2 copy-start.33
  205.8 4.2 copy-start.15
  210.0 2.3 copy-start.37
  212.3 48.6 %copy-start.45 = (f32[128]{0:T(128)}, f32[128]{0:T(128)S(1)}, u32[]{:S(2)}) copy-start(f32[128]{0:T(128)S(1)} %get-tuple-element.588) | copy-start | bytes 1540
  212.3 48.6 %copy-start.42 = (f32[128]{0:T(128)}, f32[128]{0:T(128)S(1)}, u32[]{:S(2)}) copy-start(f32[128]{0:T(128)S(1)} %fusion.107) | copy-start | bytes 1540
  264.6 108.2 %copy-start.17 = (bf16[1,256,960]{1,2,0:T(8,128)(2,1)S(1)}, bf16[1,256,960]{1,2,0:T(8,128)(2,1)}, u32[]{:S(2)}) copy-start(bf16[1,256,960]{1,2,0:T(8,128)(2,1)} %all-gather.1) | copy-start | bytes 1474564
  372.8 4.9 copy-start.3
  377.7 2.2 copy-start.2
  382.1 18.2 %reduce-scatter.51.cloned.1.call-start = ((), (), s32[]{:S(2)}) async-start(), calls=%async_computation.24 | async-start | bytes 786432
  386.3 121.8 %reduce-scatter.55.cloned.1.call-start = ((), (), s32[]{:S(2)}) async-start(), calls=%async_computation.26 | async-start | bytes 1671168
  401.4 1.8 copy-start.1
  401.5 2.7 copy-start.20
  403.2 1.6 copy-start.34
  447.3 123.3 %reduce-scatter.57.cloned.1.call-start = ((), (), s32[]{:S(2)}) async-start(), calls=%async_computation.27 | async-start | bytes 1671168
  451.1 2.7 copy-start.14
  453.7 228.4 %reduce-scatter.45.cloned.1.call-start = ((), (), s32[]{:S(2)}) async-start(), calls=%async_computation.19 | async-start | bytes 2949120 | tf_op jit(solution)/shard_map/reduce_scatter | solution.py:385
  456.3 283.6 %reduce-scatter.47.cloned.1.call-start = ((), (), s32[]{:S(2)}) async-start(), calls=%async_computation.20 | async-start | bytes 2949120 | tf_op jit(solution)/shard_map/reduce_scatter | solution.py:388
  459.8 352.6 %reduce-scatter.49.cloned.1.call-start = ((), (), s32[]{:S(2)}) async-start(), calls=%async_computation.21 | async-start | bytes 2949120 | tf_op jit(solution)/shard_map/reduce_scatter | solution.py:391
  463.4 2.9 copy-start.5
  463.4 2.9 copy-start.16
  463.5 394.0 %reduce-scatter.61.cloned.1.call-start = ((), (), s32[]{:S(2)}) async-start(), calls=%async_computation.29 | async-start | bytes 368640
  572.0 98.7 %copy-start.46 = (u32[32]{0:T(128)S(1)}, u32[32]{0:T(128)}, u32[]{:S(2)}) copy-start(u32[32]{0:T(128)} %constant.125) | copy-start | bytes 388
  648.1 23.9 %collective-permute-start.1 = (bf16[24,960]{1,0:T(8,128)(2,1)S(1)}, bf16[24,960]{1,0:T(8,128)(2,1)S(1)}, u32[]{:S(2)}, u32[]{:S(2)}) collective-permute-start(bf16[24,960]{1,0:T(8,128)(2,1)S(1)} %get-tuple-element.555), channel_id=1, source_target_pairs={{0,1},{1,2},{2,3},{3,4},{4,5},{5,6},{6,7},{7,8},{8,9},{9,10},{10,1... | collective-permute-start | bytes 138248
  657.1 16.3 %collective-permute-start.2 = (bf16[24,960]{1,0:T(8,128)(2,1)S(1)}, bf16[24,960]{1,0:T(8,128)(2,1)S(1)}, u32[]{:S(2)}, u32[]{:S(2)}) collective-permute-start(bf16[24,960]{1,0:T(8,128)(2,1)S(1)} %get-tuple-element.555), channel_id=1, source_target_pairs={{0,2},{1,3},{2,4},{3,5},{4,6},{5,7},{6,8},{7,9},{8,10},{9,11},{10,... | collective-permute-start | bytes 138248
  661.3 7.5 collective-permute-start.3
  664.6 12.5 %collective-permute-start.4 = (bf16[24,960]{1,0:T(8,128)(2,1)S(1)}, bf16[24,960]{1,0:T(8,128)(2,1)S(1)}, u32[]{:S(2)}, u32[]{:S(2)}) collective-permute-start(bf16[24,960]{1,0:T(8,128)(2,1)S(1)} %get-tuple-element.556), channel_id=1, source_target_pairs={{0,1},{1,2},{2,3},{3,4},{4,5},{5,6},{6,7},{7,8},{8,9},{9,10},{10,1... | collective-permute-start | bytes 138248
  665.9 11.2 %collective-permute-start.5 = (bf16[24,960]{1,0:T(8,128)(2,1)S(1)}, bf16[24,960]{1,0:T(8,128)(2,1)S(1)}, u32[]{:S(2)}, u32[]{:S(2)}) collective-permute-start(bf16[24,960]{1,0:T(8,128)(2,1)S(1)} %get-tuple-element.556), channel_id=1, source_target_pairs={{0,2},{1,3},{2,4},{3,5},{4,6},{5,7},{6,8},{7,9},{8,10},{9,11},{10,... | collective-permute-start | bytes 138248
  668.8 8.3 collective-permute-start.6
  672.0 7.6 collective-permute-start
  673.4 6.4 collective-permute-start.7
  678.6 180.5 %reduce-scatter.63.cloned.1.call-start = ((), (), s32[]{:S(2)}) async-start(), calls=%async_computation.30 | async-start | bytes 368640
  679.5 181.2 %reduce-scatter.59.cloned.1.call-start = ((), (), s32[]{:S(2)}) async-start(), calls=%async_computation.28 | async-start | bytes 368640
  680.2 61.7 %copy-start.7 = (bf16[16,20,960]{2,1,0:T(8,128)(2,1)S(1)}, bf16[16,20,960]{2,1,0:T(8,128)(2,1)}, u32[]{:S(2)}) copy-start(bf16[16,20,960]{2,1,0:T(8,128)(2,1)} %copy-done.6) | copy-start | bytes 1843204
  681.1 187.0 %reduce-scatter.65.cloned.1.call-start = ((), (), s32[]{:S(2)}) async-start(), calls=%async_computation.31 | async-start | bytes 368640
  682.1 202.6 %reduce-scatter.67.cloned.1.call-start = ((), (), s32[]{:S(2)}) async-start(), calls=%async_computation.32 | async-start | bytes 737280
  684.2 216.8 %reduce-scatter.69.cloned.1.call-start = ((), (), s32[]{:S(2)}) async-start(), calls=%async_computation.33 | async-start | bytes 737280
  741.8 175.7 %reduce-scatter.71.cloned.1.call-start = ((), (), s32[]{:S(2)}) async-start(), calls=%async_computation.34 | async-start | bytes 737280
  742.2 4.5 copy-start.12
  742.2 4.5 copy-start.25
  814.4 2.6 copy-start.41
  814.4 42.1 %copy-start.44 = (f32[128]{0:T(128)S(1)}, f32[128]{0:T(128)}, u32[]{:S(2)}) copy-start(f32[128]{0:T(128)} %copy-done.43) | copy-start | bytes 1540
  (18 other events, 19.5 us)
Sparse Core Ops, SparseCore 0:
  42.4 36.2 all-gather.20
  81.5 37.2 all-gather.22
  121.5 40.5 all-gather.30
  164.6 40.0 all-gather.32
  207.3 53.5 all-gather.24
  263.5 53.2 all-gather.26
  319.5 53.2 all-gather.28
  382.3 6.5 reduce-scatter.52
  391.2 9.0 reduce-scatter.50
  447.4 60.5 reduce-scatter.54
  512.1 58.4 reduce-scatter.56
  574.0 91.3 reduce-scatter.44
  668.9 70.8 reduce-scatter.46
  743.2 69.1 reduce-scatter.48
  815.0 10.8 reduce-scatter.60
  828.6 11.2 reduce-scatter.62
  842.6 11.7 reduce-scatter.58
  856.5 11.6 reduce-scatter.64
  870.4 14.1 reduce-scatter.66
  886.8 14.1 reduce-scatter.68
  903.3 14.1 reduce-scatter.70
where the time goes:
time: 934 us; the launch traced here: 926 us
  waiting for transfers between devices  460 us (49%)
  blocking collectives  223 us (24%)
  matrix products  76.4 us (8%)
  local copies, waits for them, and re-layouts  75.1 us (8%)
  other arithmetic  31.5 us (3%)
  starting transfers between devices  28.4 us (3%)
  loops' own time  16.2 us (2%)
  between operations  16.2 us (2%)
    unnamed x40, waiting for transfers between devices  161 us
    unnamed x1, blocking collectives  76.1 us
    reduce_scatter x1, waiting for transfers between devices, body(): lax.psum_scatter(grad_down.astype(jnp.bfloat16), 'context', scatter_dimen...  65.2 us
    reduce_scatter x1, waiting for transfers between devices, body(): lax.psum_scatter(grad_up_w.astype(jnp.bfloat16), 'context', scatter_dimen...  55.6 us
    all_gather x1, waiting for transfers between devices, gather_weights(): lax.all_gather(down_w, 'context', axis=0, tiled=True)  52.3 us
    all_gather x1, waiting for transfers between devices, gather_weights(): lax.all_gather(up_w, 'context', axis=0, tiled=True)  52.2 us
    unnamed x135, local copies, waits for them, and re-layouts  50.3 us
    all_gather x1, waiting for transfers between devices, gather_weights(): lax.all_gather(gate_w, 'context', axis=0, tiled=True)  46 us
  transfers between devices with their start and end apart: 29, of which 14 were waited for; matrix products, arithmetic and copies ran while one was open for 21% of the time, Pallas kernels for 0%

commit v1 on v0

v1 whole, which is shorter than its diff:
```python
import functools
import itertools

import jax
import jax.numpy as jnp
from jax import lax
from jax.experimental import pallas as pl
from jax.experimental.pallas import tpu as pltpu
from jax.sharding import PartitionSpec as P

QUERY_HEAD_COUNT = 15
KEY_VALUE_HEADS = 5
HEAD_WIDTH = 64
GROUP = QUERY_HEAD_COUNT // KEY_VALUE_HEADS
SLOT_ORDER = ("shard", "hi", "lo", "tensor")
VMEM_LIMIT = 50 * 1024 * 1024

epsilon = 1e-05


class Grid:
    def __init__(self, mesh):
        context = mesh.shape["context"]
        hi = 4 if context % 4 == 0 else 1
        self.size = {
            "shard": mesh.shape["shard"],
            "hi": hi,
            "lo": context // hi,
            "tensor": mesh.shape["tensor"],
        }

    def here(self):
        context = lax.axis_index("context")
        return {
            "shard": lax.axis_index("shard"),
            "hi": context // self.size["lo"],
            "lo": context % self.size["lo"],
            "tensor": lax.axis_index("tensor"),
        }

    def peer(self, me, axis, offset):
        there = (me[axis] + offset) % self.size[axis]
        if axis == "hi":
            return {"context": there * self.size["lo"] + me["lo"]}
        if axis == "lo":
            return {"context": me["hi"] * self.size["lo"] + there}
        return {axis: there}

    def slot(self, me, stages, offsets):
        place = dict(zip(stages, offsets))
        index = 0
        for axis in SLOT_ORDER:
            if axis in place:
                there = (me[axis] + place[axis]) % self.size[axis] if place[axis] else me[axis]
                index = index * self.size[axis] + there
        return index

    def count(self, stages):
        total = 1
        for axis in stages:
            total *= self.size[axis]
        return total


def greet(grid, me, axes):
    barrier = pltpu.get_barrier_semaphore()
    total = 0
    for axis in axes:
        for offset in range(1, grid.size[axis]):
            pl.semaphore_signal(
                barrier,
                inc=1,
                device_id=grid.peer(me, axis, offset),
                device_id_type=pl.DeviceIdType.MESH,
            )
            total += 1
    pl.semaphore_wait(barrier, total)


def remote(source, target, send, receive, device):
    return pltpu.make_async_remote_copy(
        src_ref=source,
        dst_ref=target,
        send_sem=send,
        recv_sem=receive,
        device_id=device,
        device_id_type=pl.DeviceIdType.MESH,
    )


def arrival(offsets):
    return max([at for at, offset in enumerate(offsets) if offset], default=-1)


def gather_sends(grid, stages):
    total = 0
    for offsets in itertools.product(*[range(grid.size[axis]) for axis in stages]):
        for axis in stages[arrival(offsets) + 1 :]:
            total += grid.size[axis] - 1
    return total


def flat_index(sizes, offsets):
    index = 0
    for size, offset in zip(sizes, offsets):
        index = index * size + offset
    return index


def gather_kernel(grid, plans, *refs):
    number = len(plans)
    sources, targets = refs[:number], refs[number : 2 * number]
    sems = refs[2 * number :]
    me = grid.here()
    greet(grid, me, [axis for axis in SLOT_ORDER if any(axis in stages for stages in plans)])
    sent = []

    def forward(at, stages, offsets, source, used):
        target, (send, receive, unused) = targets[at], sems[3 * at : 3 * at + 3]
        sizes = [grid.size[axis] for axis in stages]
        slot = grid.slot(me, stages, offsets)
        for stage in range(arrival(offsets) + 1, len(stages)):
            for step in range(1, sizes[stage]):
                landing = list(offsets)
                landing[stage] = (-step) % sizes[stage]
                copy = remote(
                    source,
                    target.at[slot],
                    send.at[used],
                    receive.at[flat_index(sizes, landing)],
                    grid.peer(me, stages[stage], step),
                )
                copy.start()
                sent.append(copy)
                used += 1
        return used

    used = [0] * number
    own = []
    for at, stages in enumerate(plans):
        none = (0,) * len(stages)
        used[at] = forward(at, stages, none, sources[at], used[at])
        copy = pltpu.make_async_copy(
            sources[at], targets[at].at[grid.slot(me, stages, none)], sems[3 * at + 2]
        )
        copy.start()
        own.append(copy)
    for at, stages in enumerate(plans):
        sizes = [grid.size[axis] for axis in stages]
        order = sorted(
            itertools.product(*[range(size) for size in sizes]),
            key=lambda offsets: (arrival(offsets), offsets),
        )
        for offsets in order:
            if arrival(offsets) < 0:
                continue
            block = targets[at].at[grid.slot(me, stages, offsets)]
            last = arrival(offsets)
            remote(
                block,
                block,
                sems[3 * at].at[0],
                sems[3 * at + 1].at[flat_index(sizes, offsets)],
                grid.peer(me, stages[last], offsets[last]),
            ).wait_recv()
            used[at] = forward(at, stages, offsets, block, used[at])
    for copy in sent:
        copy.wait_send()
    for copy in own:
        copy.wait()


def gather_blocks(grid, identity, arrays, plans):
    scratch = []
    for stages in plans:
        scratch += [
            pltpu.SemaphoreType.DMA((gather_sends(grid, stages),)),
            pltpu.SemaphoreType.DMA((grid.count(stages),)),
            pltpu.SemaphoreType.DMA,
        ]
    bytes_moved = sum(
        2 * grid.count(stages) * array.size * array.dtype.itemsize
        for array, stages in zip(arrays, plans)
    )
    return pl.pallas_call(
        functools.partial(gather_kernel, grid, plans),
        out_shape=[
            jax.ShapeDtypeStruct((grid.count(stages), *array.shape), array.dtype)
            for array, stages in zip(arrays, plans)
        ],
        in_specs=[pl.BlockSpec(memory_space=pl.ANY)] * len(plans),
        out_specs=[pl.BlockSpec(memory_space=pl.ANY)] * len(plans),
        scratch_shapes=scratch,
        compiler_params=pltpu.CompilerParams(collective_id=identity, has_side_effects=True),
        cost_estimate=pl.CostEstimate(
            flops=0, bytes_accessed=bytes_moved * 8, transcendentals=0
        ),
        name=f"gather_blocks_{identity}",
    )(*arrays)


def rest_count(grid, stages, stage):
    return (grid.size[stages[stage]] - 1) * grid.count(stages[stage + 1 :])


def rest_index(grid, stages, stage, offsets):
    index = offsets[stage] - 1
    for at in range(stage + 1, len(stages)):
        index = index * grid.size[stages[at]] + offsets[at]
    return index


def scatter_kernel(grid, plans, with_gains, *refs):
    number = len(plans)
    extra = 1 if with_gains else 0
    sources = refs[: number + extra]
    targets = refs[number + extra : 2 * (number + extra)]
    scratch = list(refs[2 * (number + extra) :])
    me = grid.here()
    greet(
        grid,
        me,
        [
            axis
            for axis in SLOT_ORDER
            if with_gains or any(axis in stages for stages in plans)
        ],
    )
    sent = []
    tasks = []
    for stages in plans:
        landing, leaving, send, receive = [], [None], [], []
        for stage in range(len(stages)):
            landing.append(scratch.pop(0))
            if stage:
                leaving.append(scratch.pop(0))
            send.append(scratch.pop(0))
            receive.append(scratch.pop(0))
        tasks.append((landing, leaving, send, receive))

    def pick(at, stages, stage):
        choices = [[0]] * stage + [range(1, grid.size[stages[stage]])]
        for axis in stages[stage + 1 :]:
            choices.append([*range(1, grid.size[axis]), 0])
        later = list(itertools.product(*choices))
        return sorted(later, key=lambda offsets: [offset == 0 for offset in reversed(offsets)])

    def push(at, stages, stage, offsets, source):
        landing, leaving, send, receive = tasks[at]
        index = rest_index(grid, stages, stage, offsets)
        copy = remote(
            source,
            landing[stage].at[index],
            send[stage].at[index],
            receive[stage].at[index],
            grid.peer(me, stages[stage], offsets[stage]),
        )
        copy.start()
        sent.append(copy)

    def total(at, stages, stage, offsets):
        landing, leaving, send, receive = tasks[at]
        parts = []
        for before in range(stage):
            for step in range(1, grid.size[stages[before]]):
                place = list(offsets)
                place[before] = step
                index = rest_index(grid, stages, before, place)
                block = landing[before].at[index]
                remote(
                    block,
                    block,
                    send[before].at[index],
                    receive[before].at[index],
                    grid.peer(me, stages[before], step),
                ).wait_recv()
                parts.append(block)
        amount = sources[at][grid.slot(me, stages, offsets)].astype(jnp.float32)
        for block in parts:
            amount = amount + block[...].astype(jnp.float32)
        return amount

    for at, stages in enumerate(plans):
        for offsets in pick(at, stages, 0):
            push(at, stages, 0, offsets, sources[at].at[grid.slot(me, stages, offsets)])
    if with_gains:
        amount = sources[number][...]
        for axis in ("tensor", "shard", "lo", "hi"):
            held, send, receive = scratch.pop(0), scratch.pop(0), scratch.pop(0)
            held[me[axis]] = amount
            copies = []
            for step in range(1, grid.size[axis]):
                copy = remote(
                    held.at[me[axis]],
                    held.at[me[axis]],
                    send.at[step - 1],
                    receive.at[step - 1],
                    grid.peer(me, axis, step),
                )
                copy.start()
                copies.append(copy)
            for step in range(1, grid.size[axis]):
                block = held.at[(me[axis] - step) % grid.size[axis]]
                remote(
                    block,
                    block,
                    send.at[step - 1],
                    receive.at[step - 1],
                    grid.peer(me, axis, step),
                ).wait_recv()
            amount = held[0]
            for index in range(1, grid.size[axis]):
                amount = amount + held[index]
            sent += copies
        targets[number][...] = amount
    for at, stages in enumerate(plans):
        for stage in range(1, len(stages)):
            for offsets in pick(at, stages, stage):
                leaving = tasks[at][1][stage].at[rest_index(grid, stages, stage, offsets)]
                leaving[...] = total(at, stages, stage, offsets).astype(leaving.dtype)
                push(at, stages, stage, offsets, leaving)
        targets[at][...] = total(at, stages, len(stages), (0,) * len(stages))
    for copy in sent:
        copy.wait_send()


def scatter_sums(grid, identity, arrays, plans, gains=None):
    scratch = []
    for array, stages in zip(arrays, plans):
        for stage in range(len(stages)):
            count = rest_count(grid, stages, stage)
            scratch.append(pltpu.VMEM((count, *array.shape[1:]), array.dtype))
            if stage:
                scratch.append(pltpu.VMEM((count, *array.shape[1:]), array.dtype))
            scratch += [pltpu.SemaphoreType.DMA((count,)), pltpu.SemaphoreType.DMA((count,))]
    outs = [jax.ShapeDtypeStruct(array.shape[1:], jnp.float32) for array in arrays]
    operands = list(arrays)
    if gains is not None:
        for axis in ("tensor", "shard", "lo", "hi"):
            size = grid.size[axis]
            scratch += [
                pltpu.VMEM((size, *gains.shape), gains.dtype),
                pltpu.SemaphoreType.DMA((max(size - 1, 1),)),
                pltpu.SemaphoreType.DMA((max(size - 1, 1),)),
            ]
        operands.append(gains)
        outs.append(jax.ShapeDtypeStruct(gains.shape, gains.dtype))
    bytes_moved = sum(2 * array.size * array.dtype.itemsize for array in arrays)
    return pl.pallas_call(
        functools.partial(scatter_kernel, grid, plans, gains is not None),
        out_shape=outs,
        in_specs=[pl.BlockSpec(memory_space=pltpu.VMEM)] * len(operands),
        out_specs=[pl.BlockSpec(memory_space=pltpu.VMEM)] * len(operands),
        scratch_shapes=scratch,
        compiler_params=pltpu.CompilerParams(
            collective_id=identity, has_side_effects=True, vmem_limit_bytes=VMEM_LIMIT
        ),
        cost_estimate=pl.CostEstimate(
            flops=0, bytes_accessed=bytes_moved * 8, transcendentals=0
        ),
        name=f"scatter_sums_{identity}",
    )(*operands)


def dot_last(left, right):
    return lax.dot_general(left, right, (((1,), (1,)), ((), ())), preferred_element_type=jnp.float32)


def dot_plain(left, right):
    return lax.dot_general(left, right, (((1,), (0,)), ((), ())), preferred_element_type=jnp.float32)


def attend_kernel(queries, keys, values, bias, mixed, norms):
    scores = dot_last(keys[0], queries[0]) + bias[...]
    highest = jnp.max(scores, axis=0, keepdims=True)
    weights = jnp.exp(scores - highest)
    sums = jnp.sum(weights, axis=0, keepdims=True)
    probs = (weights * (1.0 / sums)).astype(jnp.bfloat16)
    mixed[0] = dot_plain(values[0].T, probs).T.astype(mixed.dtype)
    norms[0] = highest + jnp.log(sums)


def attend_back_kernel(queries, keys, values, bias, norms, gradient, grad_q, grad_k, grad_v):
    scores = dot_last(keys[0], queries[0]) + bias[...]
    probs = jnp.exp(scores - norms[0])
    grad_probs = dot_last(values[0], gradient[0])
    delta = jnp.sum(probs * grad_probs, axis=0, keepdims=True)
    grad_scores = (probs * (grad_probs - delta)).astype(jnp.bfloat16)
    grad_q[0] = dot_plain(keys[0].T, grad_scores).T * HEAD_WIDTH ** (-0.5)
    grad_k[0] = dot_plain(grad_scores, queries[0]).astype(grad_k.dtype)
    grad_v[0] = dot_plain(probs.astype(jnp.bfloat16), gradient[0]).astype(grad_v.dtype)


def per_head(rows, columns):
    return pl.BlockSpec((1, rows, columns), lambda head: (head, 0, 0))


def attend(queries, keys, values, bias):
    total, rows = keys.shape[1], queries.shape[1]
    return pl.pallas_call(
        attend_kernel,
        grid=(KEY_VALUE_HEADS,),
        in_specs=[
            per_head(rows, HEAD_WIDTH),
            per_head(total, HEAD_WIDTH),
            per_head(total, HEAD_WIDTH),
            pl.BlockSpec((total, rows), lambda head: (0, 0)),
        ],
        out_specs=[per_head(rows, HEAD_WIDTH), per_head(1, rows)],
        out_shape=[
            jax.ShapeDtypeStruct((KEY_VALUE_HEADS, rows, HEAD_WIDTH), jnp.bfloat16),
            jax.ShapeDtypeStruct((KEY_VALUE_HEADS, 1, rows), jnp.float32),
        ],
        compiler_params=pltpu.CompilerParams(vmem_limit_bytes=VMEM_LIMIT),
        name="attend",
    )(queries, keys, values, bias)


def attend_back(queries, keys, values, bias, norms, gradient):
    total, rows = keys.shape[1], queries.shape[1]
    return pl.pallas_call(
        attend_back_kernel,
        grid=(KEY_VALUE_HEADS,),
        in_specs=[
            per_head(rows, HEAD_WIDTH),
            per_head(total, HEAD_WIDTH),
            per_head(total, HEAD_WIDTH),
            pl.BlockSpec((total, rows), lambda head: (0, 0)),
            per_head(1, rows),
            per_head(rows, HEAD_WIDTH),
        ],
        out_specs=[
            per_head(rows, HEAD_WIDTH),
            per_head(total, HEAD_WIDTH),
            per_head(total, HEAD_WIDTH),
        ],
        out_shape=[
            jax.ShapeDtypeStruct((KEY_VALUE_HEADS, rows, HEAD_WIDTH), jnp.float32),
            jax.ShapeDtypeStruct((KEY_VALUE_HEADS, total, HEAD_WIDTH), jnp.bfloat16),
            jax.ShapeDtypeStruct((KEY_VALUE_HEADS, total, HEAD_WIDTH), jnp.bfloat16),
        ],
        compiler_params=pltpu.CompilerParams(vmem_limit_bytes=VMEM_LIMIT),
        name="attend_back",
    )(queries, keys, values, bias, norms, gradient)


def rms_scale(value_matrix, gain):
    return (
        value_matrix
        * lax.rsqrt(jnp.mean(value_matrix * value_matrix, axis=-1, keepdims=True) + epsilon)
        * gain
    )


def apply_rotation(value_matrix, slot_positions, heads, direction):
    head_size = value_matrix.shape[1] // heads
    half_dim = head_size // 2
    freqs = 10000.0 ** (-jnp.arange(half_dim, dtype=jnp.float32) / half_dim)
    angles = slot_positions.astype(jnp.float32)[:, None] * freqs[None, :]
    cosine = jnp.cos(angles)[:, None, :]
    sine = direction * jnp.sin(angles)[:, None, :]
    split_heads = value_matrix.reshape(value_matrix.shape[0], heads, head_size)
    first_half = split_heads[..., :half_dim]
    second_half = split_heads[..., half_dim:]
    turned = jnp.concatenate(
        [first_half * cosine - second_half * sine, second_half * cosine + first_half * sine],
        axis=-1,
    )
    return turned.reshape(value_matrix.shape)


GATHER_PART = ("hi", "lo", "tensor")
GATHER_ALL = ("hi", "lo", "shard", "tensor")
SCATTER_PART = ("tensor", "lo", "hi")
SCATTER_ALL = ("tensor", "shard", "lo", "hi")


def to_groups(rows):
    count = rows.shape[0]
    split = rows.reshape(count, KEY_VALUE_HEADS, GROUP, HEAD_WIDTH)
    return split.transpose(1, 2, 0, 3).reshape(KEY_VALUE_HEADS, GROUP * count, HEAD_WIDTH)


def from_groups(groups):
    count = groups.shape[1] // GROUP
    split = groups.reshape(KEY_VALUE_HEADS, GROUP, count, HEAD_WIDTH)
    return split.transpose(2, 0, 1, 3).reshape(count, QUERY_HEAD_COUNT * HEAD_WIDTH)


def body(
    grid,
    tokens,
    positions,
    gain_one,
    w_query,
    key_weight,
    value_weight,
    w_out,
    gain_two,
    w_gate,
    w_up,
    w_down,
    cotangent,
):
    shards = grid.size["shard"]
    devices = grid.count(GATHER_PART)
    inputs = tokens[0].astype(jnp.float32)
    slot_positions = positions[0]
    incoming = cotangent[0].astype(jnp.float32)
    count = inputs.shape[0]
    width = inputs.shape[1]
    part = width // shards
    q_rows, k_rows, units = w_query.shape[0], key_weight.shape[0], w_gate.shape[0]
    kv_width = KEY_VALUE_HEADS * HEAD_WIDTH
    total_rows = devices * count

    cot_all = lax.all_gather(cotangent[0], ("context", "tensor"), axis=0, tiled=True)
    packed = jnp.concatenate([w_query, key_weight, value_weight, w_out], axis=0)
    (attention_blocks,) = gather_blocks(grid, 1, [packed], [GATHER_ALL])
    attention_w = attention_blocks.reshape(shards, devices, packed.shape[0], part)
    attention_w = attention_w.transpose(1, 2, 0, 3).reshape(devices, packed.shape[0], width)
    q_end, k_end, v_end = q_rows, q_rows + k_rows, q_rows + 2 * k_rows
    query_w = attention_w[:, :q_end].reshape(devices * q_rows, width)
    key_w = attention_w[:, q_end:k_end].reshape(devices * k_rows, width)
    value_w = attention_w[:, k_end:v_end].reshape(devices * k_rows, width)
    out_w = attention_w[:, v_end:].reshape(devices * q_rows, width)

    normed_one = rms_scale(inputs, gain_one).astype(jnp.bfloat16)
    queries = dot_last(normed_one, query_w)
    key_matrix = dot_last(normed_one, key_w)
    value_matrix = dot_last(normed_one, value_w).astype(jnp.bfloat16)
    rotated_queries = apply_rotation(queries, slot_positions, QUERY_HEAD_COUNT, 1.0).astype(
        jnp.bfloat16
    )
    rotated_keys = apply_rotation(key_matrix, slot_positions, KEY_VALUE_HEADS, 1.0).astype(
        jnp.bfloat16
    )
    block_number = (slot_positions[0] // count).astype(jnp.bfloat16)
    pack = jnp.concatenate([rotated_keys, value_matrix], axis=1)
    pack = jnp.concatenate([pack, jnp.broadcast_to(block_number, (16, 2 * kv_width))], axis=0)
    units_w = jnp.concatenate([w_gate, w_up, w_down], axis=0)
    gathered, units_blocks = gather_blocks(
        grid, 2, [pack, units_w], [GATHER_PART, ("shard",)]
    )
    block_numbers = gathered[:, count, 0].astype(jnp.int32)
    key_places = (block_numbers[:, None] * count + jnp.arange(count)[None, :]).reshape(total_rows)
    query_places = jnp.tile(slot_positions, GROUP)
    bias = jnp.where(key_places[:, None] <= query_places[None, :], 0.0, -1e30).astype(jnp.float32)
    by_head = gathered[:, :count].reshape(total_rows, 2, KEY_VALUE_HEADS, HEAD_WIDTH)
    by_head = by_head.transpose(1, 2, 0, 3)
    all_keys, all_values = by_head[0], by_head[1]
    grouped_queries = to_groups(rotated_queries) * jnp.bfloat16(HEAD_WIDTH ** (-0.5))
    mixed, norms = attend(grouped_queries, all_keys, all_values, bias)
    mixed_low = from_groups(mixed)

    middle = inputs + dot_last(mixed_low, out_w)
    normed_two = rms_scale(middle, gain_two).astype(jnp.bfloat16)
    (normed_blocks,) = gather_blocks(grid, 3, [normed_two], [GATHER_PART])
    normed_all = normed_blocks.reshape(total_rows, width)
    units_full = units_blocks.transpose(1, 0, 2).reshape(3 * units, width)
    gate_up = units_full[: 2 * units]
    down_w = units_full[2 * units :]
    gates_lifted = dot_last(normed_all, gate_up)
    gates, lifted = gates_lifted[:, :units], gates_lifted[:, units:]
    grad_hidden = dot_last(cot_all, down_w)
    sigmoid = jax.nn.sigmoid(gates)
    silu = gates * sigmoid
    hidden = (silu * lifted).astype(jnp.bfloat16)
    grad_gates = (grad_hidden * lifted * sigmoid * (1.0 + gates * (1.0 - sigmoid))).astype(
        jnp.bfloat16
    )
    grad_lifted = (grad_hidden * silu).astype(jnp.bfloat16)
    grad_both = jnp.concatenate([grad_gates, grad_lifted], axis=1)
    grad_norm_part = dot_plain(grad_both, gate_up).astype(jnp.bfloat16)
    unit_part = dot_plain(hidden, down_w).astype(jnp.bfloat16)
    (grad_normed_two,) = scatter_sums(
        grid, 4, [grad_norm_part.reshape(devices, count, width)], [SCATTER_PART]
    )
    unit_out = lax.psum_scatter(
        unit_part, ("context", "tensor"), scatter_dimension=0, tiled=True
    ).astype(jnp.float32)
    output = (middle + unit_out).astype(jnp.bfloat16)[None]

    unused_two, pull_two = jax.vjp(rms_scale, middle, gain_two)
    grad_middle_norm, grad_gain_two = pull_two(grad_normed_two)
    grad_middle = incoming + grad_middle_norm
    grad_branch = grad_middle.astype(jnp.bfloat16)
    mixed_gradient = dot_plain(grad_branch, out_w).astype(jnp.bfloat16)
    query_gradient, grad_keys, grad_values = attend_back(
        grouped_queries, all_keys, all_values, bias, norms, to_groups(mixed_gradient)
    )
    key_terms = jnp.stack([grad_keys, grad_values]).transpose(2, 0, 1, 3)
    key_terms = key_terms.reshape(devices, count, 2 * kv_width)
    grad_gate_up = jnp.dot(grad_both.T, normed_all, preferred_element_type=jnp.float32)
    grad_down = jnp.dot(hidden.T, cot_all, preferred_element_type=jnp.float32)
    grad_units = jnp.concatenate([grad_gate_up, grad_down], axis=0).astype(jnp.bfloat16)
    grad_units = grad_units.reshape(3 * units, shards, part).transpose(1, 0, 2)
    summed, unit_sums = scatter_sums(
        grid, 5, [key_terms, grad_units], [SCATTER_PART, ("shard",)]
    )
    grad_q = apply_rotation(
        from_groups(query_gradient), slot_positions, QUERY_HEAD_COUNT, -1.0
    ).astype(jnp.bfloat16)
    key_gradient = apply_rotation(
        summed[:, :kv_width], slot_positions, KEY_VALUE_HEADS, -1.0
    ).astype(jnp.bfloat16)
    grad_v = summed[:, kv_width:].astype(jnp.bfloat16)
    grad_normed_one = (
        dot_plain(grad_q, query_w) + dot_plain(key_gradient, key_w) + dot_plain(grad_v, value_w)
    )
    unused_one, pull_one = jax.vjp(rms_scale, inputs, gain_one)
    grad_inputs_norm, grad_gain_one = pull_one(grad_normed_one)
    grad_tokens = (grad_middle + grad_inputs_norm).astype(jnp.bfloat16)[None]

    def by_device(left, right):
        grad = jnp.dot(left.T, right, preferred_element_type=jnp.float32).astype(jnp.bfloat16)
        return grad.reshape(devices, grad.shape[0] // devices, shards, part)

    grads = jnp.concatenate(
        [
            by_device(grad_q, normed_one),
            by_device(key_gradient, normed_one),
            by_device(grad_v, normed_one),
            by_device(grad_branch, mixed_low),
        ],
        axis=1,
    )
    grads = grads.transpose(2, 0, 1, 3).reshape(shards * devices, packed.shape[0], part)
    gains = jnp.zeros((8, width), jnp.float32).at[0].set(grad_gain_one).at[1].set(grad_gain_two)
    sums, gain_sums = scatter_sums(grid, 6, [grads], [SCATTER_ALL], gains)
    return (
        output,
        grad_tokens,
        gain_sums[0],
        sums[:q_end],
        sums[q_end:k_end],
        sums[k_end:v_end],
        sums[v_end:],
        gain_sums[1],
        unit_sums[:units],
        unit_sums[units : 2 * units],
        unit_sums[2 * units :],
    )


def solution(mesh):
    placed = (
        P("shard", ("context", "tensor"), None),
        P("shard", ("context", "tensor")),
        P(),
        P(("context", "tensor"), "shard"),
        P(("context", "tensor"), "shard"),
        P(("context", "tensor"), "shard"),
        P(("context", "tensor"), "shard"),
        P(),
        P(("context", "tensor"), "shard"),
        P(("context", "tensor"), "shard"),
        P(("context", "tensor"), "shard"),
        P("shard", ("context", "tensor"), None),
    )
    return jax.shard_map(
        functools.partial(body, Grid(mesh)),
        mesh=mesh,
        in_specs=placed,
        out_specs=(
            P("shard", ("context", "tensor"), None),
            P("shard", ("context", "tensor"), None),
            P(),
            P(("context", "tensor"), "shard"),
            P(("context", "tensor"), "shard"),
            P(("context", "tensor"), "shard"),
            P(("context", "tensor"), "shard"),
            P(),
            P(("context", "tensor"), "shard"),
            P(("context", "tensor"), "shard"),
            P(("context", "tensor"), "shard"),
        ),
        check_vma=False,
    )
```

time: 934 us -> 549 us (0.59)
  waiting for transfers between devices: 460 us -> 14.4 us
  Pallas kernels: 0 us -> 292 us
  blocking collectives: 223 us -> 0 us
  local copies, waits for them, and re-layouts: 75.1 us -> 150 us
  matrix products: 76.4 us -> 43.6 us
  starting transfers between devices: 28.4 us -> 0.08 us
  loops' own time: 16.2 us -> 0 us
    pallas_call x0 -> x8, Pallas kernels: none -> 292 us  [the longest x3 138 us: scatter_sums(): pl.pallas_call(functools.partial(scatter_kernel, grid, plans, gains is no...]
    all_gather x7 -> x1, waiting for transfers between devices: 178 us -> 0.01 us  [body(): lax.all_gather(cotangent[0], ('context', 'tensor'), axis=0, tiled=True)]
    unnamed x40 -> x2, waiting for transfers between devices: 161 us -> 0.7 us
    reduce_scatter x3 -> x1, waiting for transfers between devices: 121 us -> 13.7 us  [body(): lax.psum_scatter(unit_part, ('context', 'tensor'), scatter_dimension=0, t...]
    all_gather x12 -> x0, blocking collectives: 107 us -> none  [the longest x1 24.4 us: gather_weights(): lax.all_gather(key_w, ('context', 'tensor'), axis=0, tiled=True)]
    unnamed x1 -> x0, blocking collectives: 76.1 us -> none
    reshape x3 -> x19, local copies, waits for them, and re-layouts: 6.47 us -> 73.9 us  [the longest x8 27.8 us: by_device(): return grad.reshape(devices, grad.shape[0] // devices, shards, part)]
    unnamed x135 -> x67, local copies, waits for them, and re-layouts: 50.3 us -> 9.49 us
  transfers between devices with their start and end apart: 29 -> 2, of which waited for: 14 -> 1; matrix products, arithmetic and copies ran while one was open for 21% -> 23% of each run, Pallas kernels for 0% -> 36%
where the time goes in v1:
time: 549 us; the launch traced here: 542 us
  Pallas kernels  292 us (53%)
  local copies, waits for them, and re-layouts  150 us (27%)
  matrix products  43.6 us (8%)
  other arithmetic  23.7 us (4%)
  between operations  17.7 us (3%)
  waiting for transfers between devices  14.4 us (3%)
    pallas_call x3, Pallas kernels, scatter_sums(): pl.pallas_call(functools.partial(scatter_kernel, grid, plans, gains is no...  138 us
    pallas_call x3, Pallas kernels, gather_blocks(): pl.pallas_call(functools.partial(gather_kernel, grid, plans), out_shape=[...  125 us
    reshape x8, local copies, waits for them, and re-layouts, by_device(): return grad.reshape(devices, grad.shape[0] // devices, shards, part)  27.8 us
    pallas_call x1, Pallas kernels, attend_back(): pl.pallas_call(attend_back_kernel, grid=(KEY_VALUE_HEADS,), in_specs=[per...  16.5 us
    dot_general x6, matrix products, dot_last(): lax.dot_general(left, right, (((1,), (1,)), ((), ())), preferred_element_...  16.4 us
    dot_general x6, matrix products, dot_plain(): lax.dot_general(left, right, (((1,), (0,)), ((), ())), preferred_element_...  15.3 us
    reduce_scatter x1, waiting for transfers between devices, body(): lax.psum_scatter(unit_part, ('context', 'tensor'), scatter_dimension=0, t...  13.7 us
    pallas_call x1, Pallas kernels, attend(): pl.pallas_call(attend_kernel, grid=(KEY_VALUE_HEADS,), in_specs=[per_head...  12.2 us
  transfers between devices with their start and end apart: 2, of which 1 were waited for; matrix products, arithmetic and copies ran while one was open for 23% of the time, Pallas kernels for 36%

profile of v1, /device:TPU:0, one launch (start us, length us, event | category | flops | bytes accessed | tf_op | source)
XLA Modules:
  0.0 541.6 jit_solution(15664238558877380299)
XLA Ops:
  11.7 1.7 pad_maximum_fusion.6.refs_0_
  13.4 47.4 %gather_blocks_1.1 = bf16[32,160,480]{2,1,0:T(8,128)(2,1)} custom-call(bf16[160,480]{1,0:T(8,128)(2,1)} %pad_maximum_fusion.6.refs_0_), custom_call_target="tpu_custom_call" | custom-call | bytes 78643200 | tf_op jit(solution)/shard_map/gather_blocks_1/pallas_call | solution.py:185
  60.8 10.3 %copy.122 = bf16[2,16,160,480]{3,0,2,1:T(2,128)(2,1)} copy(bf16[2,16,160,480]{3,2,1,0:T(8,128)(2,1)} %bitcast.163) | data formatting | bytes 9830400 | tf_op jit(solution)/shard_map/reshape | solution.py:520
  71.0 10.4 %reshape.403 = bf16[16,160,960]{2,1,0:T(8,128)(2,1)} reshape(bf16[16,160,2,480]{3,2,1,0:T(2,128)(2,1)} %bitcast.164) | data formatting | bytes 9830400 | tf_op jit(solution)/shard_map/reshape | solution.py:521
  81.4 1.8 fusion.56
  87.0 34.6 %gather_blocks_2.1 = (bf16[16,144,640]{2,1,0:T(8,128)(2,1)}, bf16[2,480,480]{2,1,0:T(8,128)(2,1)}) custom-call(bf16[144,640]{1,0:T(8,128)(2,1)} %fusion.42.refs_0_, bf16[480,480]{1,0:T(8,128)(2,1)} %pad_maximum_fusion.4.refs_1_), custom_call_target="tpu_custom_call" | custom-call | bytes 61931520 | tf_op jit(solution)/shard_map/gather_blocks_2/pallas_call | solution.py:185
  122.6 2.0 slice.177
  124.6 4.6 fusion.55
  129.2 4.0 reshape.408
  133.1 1.8 dot_general.64
  134.9 2.3 fusion.35
  138.1 1.2 copy.83
  139.3 3.6 slice.141
  142.9 4.9 copy.87
  147.8 5.2 reshape.405
  153.0 2.6 copy.91
  155.6 3.2 slice.147
  159.8 2.0 slice.151
  161.8 5.9 %copy.88 = bf16[2048,2,5,64]{3,0,2,1:T(8,128)(2,1)} copy(bf16[2048,2,5,64]{0,3,2,1:T(8,128)(2,1)} %reshape.405) | data formatting | bytes 5242880 | tf_op jit(solution)/shard_map/reshape | solution.py:549
  167.8 1.1 multiply_reduce_fusion.3
  169.0 1.9 compare_select_fusion.bias
  170.8 4.4 slice_bitcast_fusion
  175.3 12.2 %attend.1 = (bf16[5,384,64]{2,1,0:T(8,128)(2,1)S(1)}, f32[5,1,384]{2,1,0:T(1,128)S(1)}) custom-call(bf16[5,384,64]{2,1,0:T(8,128)(2,1)S(1)} %bitcast.156, bf16[5,2048,64]{2,1,0:T(8,128)(2,1)S(1)} %get-tuple-element.97.keys, bf16[5,2048,64]{2,1,0:T(8,128)(2,1)} %get-tuple-element.96.values, f32[2048,384]{1,0:T(8,128)} %compare_select_fusion.bias), custom_call_target="tpu_custom_call" | custom-call | tf_op jit(solution)/shard_map/attend/pallas_call | solution.py:400
  188.4 2.5 multiply_reduce_fusion.2
  192.5 43.3 %gather_blocks_3.1 = bf16[16,128,960]{2,1,0:T(8,128)(2,1)} custom-call(bf16[128,960]{1,0:T(8,128)(2,1)} %multiply_convert_fusion.3.refs_0_), custom_call_target="tpu_custom_call" | custom-call | bytes 62914560 | tf_op jit(solution)/shard_map/gather_blocks_3/pallas_call | solution.py:185
  235.8 5.3 fusion.61
  241.1 5.5 %multiply_convert_fusion.1 = (bf16[2048,160]{0,1:T(8,128)(2,1)}, bf16[2048,160]{0,1:T(8,128)(2,1)}, bf16[2048,160]{0,1:T(8,128)(2,1)S(1)}) fusion(f32[2048,320]{0,1:T(8,128)} %fusion.61, bf16[160,960]{1,0:T(8,128)(2,1)} %slice.151, bf16[1,2048,960]{1,2,0:T(8,128)(2,1)} %all-gather.3.cloned.1.call-done), kind=kOutput, calls=%fused_computation.21 | convolution fusion | flops 634060800 | bytes 8826880 | tf_op jit(solution)/shard_map/dot_general | solution.py:366
  246.6 3.2 convolution_convert_fusion.1
  249.8 6.4 %copy.93 = bf16[2048,960]{1,0:T(8,128)(2,1)} copy(bf16[2048,960]{0,1:T(8,128)(2,1)} %convolution_convert_fusion.1) | data formatting | bytes 7864320 | tf_op jit(solution)/shard_map/convert_element_type | solution.py:575
  256.1 1.8 copy.94
  257.9 2.2 reshape.417
  260.1 1.8 reshape.414
  261.9 6.4 %copy.99 = bf16[960,2048]{1,0:T(8,128)(2,1)} copy(bf16[960,2048]{0,1:T(8,128)(2,1)} %bitcast.166) | data formatting | bytes 7864320 | tf_op jit(solution)/shard_map/dot_general | solution.py:594
  268.3 3.6 fusion.10
  272.3 5.3 convolution_convert_fusion
  277.7 6.7 %copy.95 = bf16[2048,960]{1,0:T(8,128)(2,1)} copy(bf16[2048,960]{0,1:T(8,128)(2,1)} %convolution_convert_fusion) | data formatting | bytes 7864320 | tf_op jit(solution)/shard_map/convert_element_type | solution.py:574
  284.4 55.4 %scatter_sums_4.1 = f32[128,960]{1,0:T(8,128)S(1)} custom-call(bf16[16,128,960]{2,1,0:T(8,128)(2,1)} %bitcast.167), custom_call_target="tpu_custom_call" | custom-call | bytes 62914560 | tf_op jit(solution)/shard_map/scatter_sums_4/pallas_call | solution.py:349
  339.9 1.5 convolution_convert_fusion.6
  341.8 13.7 %reduce-scatter.2.cloned.1.call-done = bf16[128,960]{1,0:T(8,128)(2,1)} async-done(((bf16[2048,960]{1,0:T(8,128)(2,1)}), bf16[128,960]{1,0:T(8,128)(2,1)}) %reduce-scatter.2.cloned.1.call-update) | async-done | bytes 245776 | tf_op jit(solution)/shard_map/reduce_scatter | solution.py:579
  355.5 2.1 fusion.25
  358.5 2.1 convolution_convert_fusion.2
  360.9 16.5 %attend_back.1 = (f32[5,384,64]{2,1,0:T(8,128)S(1)}, bf16[5,2048,64]{2,1,0:T(8,128)(2,1)}, bf16[5,2048,64]{2,1,0:T(8,128)(2,1)}) custom-call(bf16[5,384,64]{2,1,0:T(8,128)(2,1)S(1)} %bitcast.157, bf16[5,2048,64]{2,1,0:T(8,128)(2,1)} %copy-done, bf16[5,2048,64]{2,1,0:T(8,128)(2,1)} %get-tuple-element.96.values, f32[2048,384]{1,0:T(8,128)} %compare_select_fusion.bias, ...), custom_call_target="tpu_custom_call" | custom-call | tf_op jit(solution)/shard_map/attend_back/pallas_call | solution.py:421
  377.3 6.5 %maximum_bitcast_fusion = bf16[2048,2,5,64]{3,0,2,1:T(8,128)(2,1)} fusion(bf16[1,5,2048,64]{3,2,1,0:T(8,128)(2,1)} %bitcast.172, bf16[1,5,2048,64]{3,2,1,0:T(8,128)(2,1)} %bitcast.171), kind=kLoop, calls=%fused_computation | loop fusion | flops 1310720 | bytes 5242880 | tf_op jit(solution)/shard_map/transpose | solution.py:592
  383.8 6.1 %copy.98 = bf16[2048,2,5,64]{0,3,2,1:T(8,128)(2,1)} copy(bf16[2048,2,5,64]{3,0,2,1:T(8,128)(2,1)} %maximum_bitcast_fusion) | data formatting | bytes 5242880 | tf_op jit(solution)/shard_map/transpose | solution.py:592
  389.9 4.0 copy.120
  393.9 4.8 copy.101.refs_0_
  398.8 25.1 %scatter_sums_5.1 = (f32[128,640]{1,0:T(8,128)S(1)}, f32[480,480]{1,0:T(8,128)S(1)}) custom-call(bf16[16,128,640]{2,1,0:T(8,128)(2,1)} %copy.101.refs_0_, bf16[2,480,480]{2,1,0:T(8,128)(2,1)S(1)} %maximum_bitcast_fusion.1.refs_1_), custom_call_target="tpu_custom_call" | custom-call | bytes 56688640 | tf_op jit(solution)/shard_map/scatter_sums_5/pallas_call | solution.py:349
  423.9 1.1 fusion.45
  425.7 1.3 convolution_convert_fusion.4
  427.0 1.1 copy.97
  428.1 6.6 %reshape.421 = bf16[16,60,2,480]{3,2,1,0:T(2,128)(2,1)S(1)} reshape(bf16[960,960]{1,0:T(8,128)(2,1)} %convolution_convert_fusion.2) | data formatting | bytes 3686400 | tf_op jit(solution)/shard_map/reshape | solution.py:617
  434.8 1.8 copy.109
  436.6 2.1 convolution_convert_fusion.3
  438.8 6.4 %reshape.418 = bf16[16,60,2,480]{3,2,1,0:T(2,128)(2,1)S(1)} reshape(bf16[960,960]{1,0:T(8,128)(2,1)} %convolution_convert_fusion.3) | data formatting | bytes 3686400 | tf_op jit(solution)/shard_map/reshape | solution.py:617
  445.1 1.9 copy.106
  448.1 1.2 convolution_convert_fusion.5
  449.3 2.2 fusion.62
  451.5 3.6 reshape.420
  455.2 2.1 copy.108
  457.2 3.5 reshape.419
  460.7 2.0 copy.107
  462.8 2.5 fusion.20
  465.4 6.2 %pad_maximum_fusion = bf16[16,160,2,480]{3,1,0,2:T(8,128)(2,1)} fusion(bf16[16,60,2,480]{3,1,0,2:T(8,128)(2,1)} %copy.109, bf16[16,20,2,480]{3,1,0,2:T(8,128)(2,1)} %copy.108, bf16[16,20,2,480]{3,1,0,2:T(8,128)(2,1)} %copy.107, bf16[16,60,2,480]{3,1,0,2:T(8,128)(2,1)} %copy.106), kind=kLoop, calls=%fused_computation.1 | loop fusion | flops 19660800 | bytes 9830400 | tf_op jit(solution)/shard_map/concatenate | solution.py:619
  471.6 57.8 %scatter_sums_6.1 = (f32[160,480]{1,0:T(8,128)S(1)}, f32[8,960]{1,0:T(8,128)S(1)}) custom-call(bf16[32,160,480]{2,1,0:T(8,128)(2,1)} %bitcast.162, f32[8,960]{1,0:T(8,128)S(1)} %scatter.9.refs_1_), custom_call_target="tpu_custom_call" | custom-call | bytes 78643200 | tf_op jit(solution)/shard_map/scatter_sums_6/pallas_call | solution.py:349
  (115 shorter events, 19.7 us)
Async XLA Ops:
  7.2 233.9 %all-gather.3.cloned.1.call-start = ((), (), s32[]{:S(2)}) async-start(), calls=%async_computation.2 | async-start | bytes 4177920 | tf_op jit(solution)/shard_map/all_gather | solution.py:517
  7.9 347.6 %reduce-scatter.2.cloned.1.call-start = ((), (), s32[]{:S(2)}) async-start(), calls=%async_computation.1 | async-start | bytes 4456448 | tf_op jit(solution)/shard_map/reduce_scatter | solution.py:579
  11.6 176.7 %copy-start.3 = (bf16[1,128,960]{2,1,0:T(8,128)(2,1)}, bf16[1,128,960]{2,1,0:T(8,128)(2,1)S(1)}, u32[]{:S(2)}) copy-start(bf16[1,128,960]{2,1,0:T(8,128)(2,1)S(1)} %copy.80) | copy-start | bytes 737284
  81.4 2.3 copy-start.22
  83.2 2.0 copy-start.11
  83.2 1.4 copy-start.27
  83.6 3.5 copy-start.13
  83.6 2.6 copy-start.23
  83.6 2.6 copy-start.24
  83.6 2.6 copy-start.25
  175.3 12.2 %copy-start = (bf16[5,2048,64]{2,1,0:T(8,128)(2,1)}, bf16[5,2048,64]{2,1,0:T(8,128)(2,1)S(1)}, u32[]{:S(2)}) copy-start(bf16[5,2048,64]{2,1,0:T(8,128)(2,1)S(1)} %get-tuple-element.97.keys) | copy-start | bytes 3932164
  187.4 4.2 copy-start.26
  190.8 0.8 copy-start.6
  191.6 44.1 %copy-start.20 = (bf16[320,960]{1,0:T(8,128)(2,1)S(1)}, bf16[320,960]{1,0:T(8,128)(2,1)}, u32[]{:S(2)}) copy-start(bf16[320,960]{1,0:T(8,128)(2,1)} %slice.147) | copy-start | bytes 1843204
  241.1 5.5 %copy-start.18 = (bf16[160,960]{1,0:T(8,128)(2,1)S(1)}, bf16[160,960]{1,0:T(8,128)(2,1)}, u32[]{:S(2)}) copy-start(bf16[160,960]{1,0:T(8,128)(2,1)} %slice.151) | copy-start | bytes 921604
  268.3 4.0 copy-start.21
  268.3 4.0 copy-start.28
  277.7 62.2 %copy-start.30 = (bf16[2048,160]{0,1:T(8,128)(2,1)S(1)}, bf16[2048,160]{0,1:T(8,128)(2,1)}, u32[]{:S(2)}) copy-start(bf16[2048,160]{0,1:T(8,128)(2,1)} %get-tuple-element.101) | copy-start | bytes 1966084
  284.4 55.4 %copy-start.12 = (bf16[960,2048]{1,0:T(8,128)(2,1)S(1)}, bf16[960,2048]{1,0:T(8,128)(2,1)}, u32[]{:S(2)}) copy-start(bf16[960,2048]{1,0:T(8,128)(2,1)} %copy.99) | copy-start | bytes 11796484
  284.4 55.4 %copy-start.29 = (bf16[2048,160]{0,1:T(8,128)(2,1)S(1)}, bf16[2048,160]{0,1:T(8,128)(2,1)}, u32[]{:S(2)}) copy-start(bf16[2048,160]{0,1:T(8,128)(2,1)} %get-tuple-element.100) | copy-start | bytes 1966084
  339.9 1.7 copy-start.7
  341.8 16.7 %copy-start.15 = (bf16[5,3,128,64]{2,3,1,0:T(8,128)(2,1)S(1)}, bf16[5,3,128,64]{2,3,1,0:T(8,128)(2,1)}, u32[]{:S(2)}) copy-start(bf16[5,3,128,64]{2,3,1,0:T(8,128)(2,1)} %copy.89) | copy-start | bytes 737284
  355.5 2.1 copy-start.5
  357.5 3.0 copy-start.8
  377.3 6.5 %copy-start.1 = (f32[5,384,64]{2,1,0:T(8,128)}, f32[5,384,64]{2,1,0:T(8,128)S(1)}, u32[]{:S(2)}) copy-start(f32[5,384,64]{2,1,0:T(8,128)S(1)} %get-tuple-element.50) | copy-start | bytes 1474564
  398.7 25.1 %copy-start.14 = (bf16[320,960]{1,0:T(8,128)(2,1)S(1)}, bf16[320,960]{1,0:T(8,128)(2,1)}, u32[]{:S(2)}) copy-start(bf16[320,960]{1,0:T(8,128)(2,1)} %copy-done.13) | copy-start | bytes 1843204
  398.7 26.9 %copy-start.4 = (bf16[1,128,960]{2,1,0:T(8,128)(2,1)S(1)}, bf16[1,128,960]{2,1,0:T(8,128)(2,1)}, u32[]{:S(2)}) copy-start(bf16[1,128,960]{2,1,0:T(8,128)(2,1)} %copy-done.3) | copy-start | bytes 737284
  398.8 28.2 %copy-start.2 = (f32[5,384,64]{2,1,0:T(8,128)S(1)}, f32[5,384,64]{2,1,0:T(8,128)}, u32[]{:S(2)}) copy-start(f32[5,384,64]{2,1,0:T(8,128)} %copy-done.1) | copy-start | bytes 1474564
  434.7 1.8 copy-start.17
  451.5 11.2 %copy-start.10 = (bf16[960,960]{1,0:T(8,128)(2,1)S(1)}, bf16[960,960]{1,0:T(8,128)(2,1)}, u32[]{:S(2)}) copy-start(bf16[960,960]{1,0:T(8,128)(2,1)} %reshape.414) | copy-start | bytes 5529604
  471.6 59.2 %copy-start.19 = (bf16[1,128,960]{2,1,0:T(8,128)(2,1)S(1)}, bf16[1,128,960]{2,1,0:T(8,128)(2,1)}, u32[]{:S(2)}) copy-start(bf16[1,128,960]{2,1,0:T(8,128)(2,1)} %get-tuple-element.109) | copy-start | bytes 737284
  529.4 3.2 copy-start.9
  529.4 3.2 copy-start.16
Sparse Core Ops, SparseCore 0:
  10.2 61.7 all-gather.2
  256.3 99.1 reduce-scatter.1

commit v2 on v1

--- a/solution.py
+++ b/solution.py
@@ -145,15 +145,15 @@
         )
         copy.start()
         own.append(copy)
-    for at, stages in enumerate(plans):
-        sizes = [grid.size[axis] for axis in stages]
-        order = sorted(
-            itertools.product(*[range(size) for size in sizes]),
-            key=lambda offsets: (arrival(offsets), offsets),
-        )
-        for offsets in order:
-            if arrival(offsets) < 0:
-                continue
+    for stage in range(max(len(stages) for stages in plans)):
+        everything = []
+        for at, stages in enumerate(plans):
+            choices = itertools.product(*[range(grid.size[axis]) for axis in stages])
+            listed = [offsets for offsets in choices if arrival(offsets) == stage]
+            everything += [(turn, at, offsets) for turn, offsets in enumerate(listed)]
+        for turn, at, offsets in sorted(everything):
+            stages = plans[at]
+            sizes = [grid.size[axis] for axis in stages]
             block = targets[at].at[grid.slot(me, stages, offsets)]
             last = arrival(offsets)
             remote(
@@ -313,12 +313,21 @@
                 amount = amount + held[index]
             sent += copies
         targets[number][...] = amount
-    for at, stages in enumerate(plans):
-        for stage in range(1, len(stages)):
-            for offsets in pick(at, stages, stage):
+    for stage in range(1, max(len(stages) for stages in plans)):
+        everything = []
+        for at, stages in enumerate(plans):
+            if stage < len(stages):
+                everything += [
+                    (turn, at, offsets)
+                    for turn, offsets in enumerate(pick(at, stages, stage))
+                ]
+        if everything:
+            for turn, at, offsets in sorted(everything):
+                stages = plans[at]
                 leaving = tasks[at][1][stage].at[rest_index(grid, stages, stage, offsets)]
                 leaving[...] = total(at, stages, stage, offsets).astype(leaving.dtype)
                 push(at, stages, stage, offsets, leaving)
+    for at, stages in enumerate(plans):
         targets[at][...] = total(at, stages, len(stages), (0,) * len(stages))
     for copy in sent:
         copy.wait_send()
@@ -370,78 +379,149 @@
     return lax.dot_general(left, right, (((1,), (0,)), ((), ())), preferred_element_type=jnp.float32)
 
 
+def dot_first(left, right):
+    return lax.dot_general(left, right, (((0,), (0,)), ((), ())), preferred_element_type=jnp.float32)
+
+
+def side_by_side(ref):
+    return jnp.concatenate([ref[index] for index in range(ref.shape[0])], axis=1)
+
+
+def spread(ref, amount):
+    width = ref.shape[2]
+    for index in range(ref.shape[0]):
+        ref[index] = amount[:, index * width : (index + 1) * width].astype(ref.dtype)
+
+
 def attend_kernel(queries, keys, values, bias, mixed, norms):
-    scores = dot_last(keys[0], queries[0]) + bias[...]
+    scores = dot_first(side_by_side(keys), side_by_side(queries)) + bias[...]
     highest = jnp.max(scores, axis=0, keepdims=True)
     weights = jnp.exp(scores - highest)
     sums = jnp.sum(weights, axis=0, keepdims=True)
     probs = (weights * (1.0 / sums)).astype(jnp.bfloat16)
-    mixed[0] = dot_plain(values[0].T, probs).T.astype(mixed.dtype)
+    spread(mixed, dot_plain(side_by_side(values), probs))
     norms[0] = highest + jnp.log(sums)
 
 
 def attend_back_kernel(queries, keys, values, bias, norms, gradient, grad_q, grad_k, grad_v):
-    scores = dot_last(keys[0], queries[0]) + bias[...]
+    all_queries, all_keys = side_by_side(queries), side_by_side(keys)
+    all_gradients = side_by_side(gradient)
+    scores = dot_first(all_keys, all_queries) + bias[...]
     probs = jnp.exp(scores - norms[0])
-    grad_probs = dot_last(values[0], gradient[0])
+    grad_probs = dot_first(side_by_side(values), all_gradients)
     delta = jnp.sum(probs * grad_probs, axis=0, keepdims=True)
     grad_scores = (probs * (grad_probs - delta)).astype(jnp.bfloat16)
-    grad_q[0] = dot_plain(keys[0].T, grad_scores).T * HEAD_WIDTH ** (-0.5)
-    grad_k[0] = dot_plain(grad_scores, queries[0]).astype(grad_k.dtype)
-    grad_v[0] = dot_plain(probs.astype(jnp.bfloat16), gradient[0]).astype(grad_v.dtype)
-
-
-def per_head(rows, columns):
-    return pl.BlockSpec((1, rows, columns), lambda head: (head, 0, 0))
-
-
-def attend(queries, keys, values, bias):
-    total, rows = keys.shape[1], queries.shape[1]
+    spread(grad_q, dot_plain(all_keys, grad_scores) * HEAD_WIDTH ** (-0.5))
+    spread(grad_k, dot_last(all_queries, grad_scores))
+    spread(grad_v, dot_last(all_gradients, probs.astype(jnp.bfloat16)))
+
+
+def group_spec(count):
+    return pl.BlockSpec((GROUP, HEAD_WIDTH, count), lambda head: (head, 0, 0))
+
+
+def pair_spec(blocks, count, shift):
+    return pl.BlockSpec((blocks, HEAD_WIDTH, count), lambda head: (0, head + shift, 0))
+
+
+def row_spec(rows):
+    return pl.BlockSpec((1, 1, rows), lambda head: (head, 0, 0))
+
+
+def attend(queries, pairs, bias):
+    blocks, unused, count = pairs.shape
+    rows = GROUP * count
     return pl.pallas_call(
         attend_kernel,
         grid=(KEY_VALUE_HEADS,),
         in_specs=[
-            per_head(rows, HEAD_WIDTH),
-            per_head(total, HEAD_WIDTH),
-            per_head(total, HEAD_WIDTH),
-            pl.BlockSpec((total, rows), lambda head: (0, 0)),
-        ],
-        out_specs=[per_head(rows, HEAD_WIDTH), per_head(1, rows)],
+            group_spec(count),
+            pair_spec(blocks, count, 0),
+            pair_spec(blocks, count, KEY_VALUE_HEADS),
+            pl.BlockSpec(bias.shape, lambda head: (0, 0)),
+        ],
+        out_specs=[group_spec(count), row_spec(rows)],
         out_shape=[
-            jax.ShapeDtypeStruct((KEY_VALUE_HEADS, rows, HEAD_WIDTH), jnp.bfloat16),
+            jax.ShapeDtypeStruct(queries.shape, jnp.bfloat16),
             jax.ShapeDtypeStruct((KEY_VALUE_HEADS, 1, rows), jnp.float32),
         ],
         compiler_params=pltpu.CompilerParams(vmem_limit_bytes=VMEM_LIMIT),
         name="attend",
-    )(queries, keys, values, bias)
-
-
-def attend_back(queries, keys, values, bias, norms, gradient):
-    total, rows = keys.shape[1], queries.shape[1]
+    )(queries, pairs, pairs, bias)
+
+
+def attend_back(queries, pairs, bias, norms, gradient):
+    blocks, unused, count = pairs.shape
+    rows = GROUP * count
+    grad_pair = jax.ShapeDtypeStruct((blocks, KEY_VALUE_HEADS * HEAD_WIDTH, count), jnp.bfloat16)
     return pl.pallas_call(
         attend_back_kernel,
         grid=(KEY_VALUE_HEADS,),
         in_specs=[
-            per_head(rows, HEAD_WIDTH),
-            per_head(total, HEAD_WIDTH),
-            per_head(total, HEAD_WIDTH),
-            pl.BlockSpec((total, rows), lambda head: (0, 0)),
-            per_head(1, rows),
-            per_head(rows, HEAD_WIDTH),
+            group_spec(count),
+            pair_spec(blocks, count, 0),
+            pair_spec(blocks, count, KEY_VALUE_HEADS),
+            pl.BlockSpec(bias.shape, lambda head: (0, 0)),
+            row_spec(rows),
+            group_spec(count),
         ],
         out_specs=[
-            per_head(rows, HEAD_WIDTH),
-            per_head(total, HEAD_WIDTH),
-            per_head(total, HEAD_WIDTH),
-        ],
-        out_shape=[
-            jax.ShapeDtypeStruct((KEY_VALUE_HEADS, rows, HEAD_WIDTH), jnp.float32),
-            jax.ShapeDtypeStruct((KEY_VALUE_HEADS, total, HEAD_WIDTH), jnp.bfloat16),
-            jax.ShapeDtypeStruct((KEY_VALUE_HEADS, total, HEAD_WIDTH), jnp.bfloat16),
-        ],
+            group_spec(count),
+            pair_spec(blocks, count, 0),
+            pair_spec(blocks, count, 0),
+        ],
+        out_shape=[jax.ShapeDtypeStruct(queries.shape, jnp.float32), grad_pair, grad_pair],
         compiler_params=pltpu.CompilerParams(vmem_limit_bytes=VMEM_LIMIT),
         name="attend_back",
-    )(queries, keys, values, bias, norms, gradient)
+    )(queries, pairs, pairs, bias, norms, gradient)
+
+
+def units_kernel(units, normed, cot, weights, grad_norm, unit_out, grads):
+    gate_w, up_w = weights[:units], weights[units : 2 * units]
+    down_w = weights[2 * units :]
+    rows, incoming = normed[...], cot[...]
+    gates, lifted = dot_last(rows, gate_w), dot_last(rows, up_w)
+    grad_hidden = dot_last(incoming, down_w)
+    sigmoid = jax.nn.sigmoid(gates)
+    silu = gates * sigmoid
+    hidden = (silu * lifted).astype(jnp.bfloat16)
+    grad_gates = (grad_hidden * lifted * sigmoid * (1.0 + gates * (1.0 - sigmoid))).astype(
+        jnp.bfloat16
+    )
+    grad_lifted = (grad_hidden * silu).astype(jnp.bfloat16)
+    grad_norm[...] = (dot_plain(grad_gates, gate_w) + dot_plain(grad_lifted, up_w)).astype(
+        grad_norm.dtype
+    )
+    unit_out[...] = dot_plain(hidden, down_w).astype(unit_out.dtype)
+
+    @pl.when(pl.program_id(0) == 0)
+    def clear():
+        grads[...] = jnp.zeros_like(grads)
+
+    grads[:units] += dot_first(grad_gates, rows)
+    grads[units : 2 * units] += dot_first(grad_lifted, rows)
+    grads[2 * units :] += dot_first(hidden, incoming)
+
+
+def feed_forward(normed, cot, weights):
+    total, width = normed.shape
+    rows = 256
+    units = weights.shape[0] // 3
+    by_rows = pl.BlockSpec((rows, width), lambda step: (step, 0))
+    whole = pl.BlockSpec(weights.shape, lambda step: (0, 0))
+    return pl.pallas_call(
+        functools.partial(units_kernel, units),
+        grid=(total // rows,),
+        in_specs=[by_rows, by_rows, whole],
+        out_specs=[by_rows, by_rows, whole],
+        out_shape=[
+            jax.ShapeDtypeStruct(normed.shape, jnp.bfloat16),
+            jax.ShapeDtypeStruct(normed.shape, jnp.bfloat16),
+            jax.ShapeDtypeStruct(weights.shape, jnp.float32),
+        ],
+        compiler_params=pltpu.CompilerParams(vmem_limit_bytes=VMEM_LIMIT),
+        name="feed_forward",
+    )(normed, cot, weights)
 
 
 def rms_scale(value_matrix, gain):
@@ -452,39 +532,26 @@
     )
 
 
-def apply_rotation(value_matrix, slot_positions, heads, direction):
-    head_size = value_matrix.shape[1] // heads
-    half_dim = head_size // 2
+def apply_rotation(features, slot_positions, direction):
+    half_dim = HEAD_WIDTH // 2
     freqs = 10000.0 ** (-jnp.arange(half_dim, dtype=jnp.float32) / half_dim)
-    angles = slot_positions.astype(jnp.float32)[:, None] * freqs[None, :]
-    cosine = jnp.cos(angles)[:, None, :]
-    sine = direction * jnp.sin(angles)[:, None, :]
-    split_heads = value_matrix.reshape(value_matrix.shape[0], heads, head_size)
-    first_half = split_heads[..., :half_dim]
-    second_half = split_heads[..., half_dim:]
-    turned = jnp.concatenate(
+    angles = freqs[:, None] * slot_positions.astype(jnp.float32)[None, :]
+    cosine = jnp.cos(angles)[None]
+    sine = direction * jnp.sin(angles)[None]
+    heads = features.shape[0] // HEAD_WIDTH
+    split_heads = features.reshape(heads, HEAD_WIDTH, features.shape[1])
+    first_half = split_heads[:, :half_dim]
+    second_half = split_heads[:, half_dim:]
+    return jnp.concatenate(
         [first_half * cosine - second_half * sine, second_half * cosine + first_half * sine],
-        axis=-1,
-    )
-    return turned.reshape(value_matrix.shape)
+        axis=1,
+    ).reshape(features.shape)
 
 
 GATHER_PART = ("hi", "lo", "tensor")
-GATHER_ALL = ("hi", "lo", "shard", "tensor")
+GATHER_ALL = [("hi", "lo", "shard", "tensor"), ("hi", "shard", "lo", "tensor")]
 SCATTER_PART = ("tensor", "lo", "hi")
-SCATTER_ALL = ("tensor", "shard", "lo", "hi")
-
-
-def to_groups(rows):
-    count = rows.shape[0]
-    split = rows.reshape(count, KEY_VALUE_HEADS, GROUP, HEAD_WIDTH)
-    return split.transpose(1, 2, 0, 3).reshape(KEY_VALUE_HEADS, GROUP * count, HEAD_WIDTH)
-
-
-def from_groups(groups):
-    count = groups.shape[1] // GROUP
-    split = groups.reshape(KEY_VALUE_HEADS, GROUP, count, HEAD_WIDTH)
-    return split.transpose(2, 0, 1, 3).reshape(count, QUERY_HEAD_COUNT * HEAD_WIDTH)
+SCATTER_ALL = [("tensor", "shard", "lo", "hi"), ("tensor", "lo", "shard", "hi")]
 
 
 def body(
@@ -507,75 +574,72 @@
     inputs = tokens[0].astype(jnp.float32)
     slot_positions = positions[0]
     incoming = cotangent[0].astype(jnp.float32)
-    count = inputs.shape[0]
-    width = inputs.shape[1]
+    count, width = inputs.shape
     part = width // shards
     q_rows, k_rows, units = w_query.shape[0], key_weight.shape[0], w_gate.shape[0]
+    both = q_rows + k_rows
     kv_width = KEY_VALUE_HEADS * HEAD_WIDTH
     total_rows = devices * count
+    flat = devices * both
+
+    def columns(rows):
+        return [rows[:, at * part : (at + 1) * part] for at in range(shards)]
+
+    def sum_halves(weights, halves, dot):
+        total = dot(weights[0], halves[0])
+        for at in range(1, shards):
+            total = total + dot(weights[at], halves[at])
+        return total.reshape(devices, both, count)
 
     cot_all = lax.all_gather(cotangent[0], ("context", "tensor"), axis=0, tiled=True)
-    packed = jnp.concatenate([w_query, key_weight, value_weight, w_out], axis=0)
-    (attention_blocks,) = gather_blocks(grid, 1, [packed], [GATHER_ALL])
-    attention_w = attention_blocks.reshape(shards, devices, packed.shape[0], part)
-    attention_w = attention_w.transpose(1, 2, 0, 3).reshape(devices, packed.shape[0], width)
-    q_end, k_end, v_end = q_rows, q_rows + k_rows, q_rows + 2 * k_rows
-    query_w = attention_w[:, :q_end].reshape(devices * q_rows, width)
-    key_w = attention_w[:, q_end:k_end].reshape(devices * k_rows, width)
-    value_w = attention_w[:, k_end:v_end].reshape(devices * k_rows, width)
-    out_w = attention_w[:, v_end:].reshape(devices * q_rows, width)
+    first_blocks, second_blocks = gather_blocks(
+        grid,
+        1,
+        [
+            jnp.concatenate([w_query, key_weight], axis=0),
+            jnp.concatenate([value_weight, w_out], axis=0),
+        ],
+        GATHER_ALL,
+    )
+    first_w = first_blocks.reshape(shards, flat, part)
+    second_w = second_blocks.reshape(shards, flat, part)
 
     normed_one = rms_scale(inputs, gain_one).astype(jnp.bfloat16)
-    queries = dot_last(normed_one, query_w)
-    key_matrix = dot_last(normed_one, key_w)
-    value_matrix = dot_last(normed_one, value_w).astype(jnp.bfloat16)
-    rotated_queries = apply_rotation(queries, slot_positions, QUERY_HEAD_COUNT, 1.0).astype(
-        jnp.bfloat16
-    )
-    rotated_keys = apply_rotation(key_matrix, slot_positions, KEY_VALUE_HEADS, 1.0).astype(
-        jnp.bfloat16
-    )
+    normed_halves = columns(normed_one)
+    first = sum_halves(first_w, normed_halves, dot_last)
+    second = sum_halves(second_w, normed_halves, dot_last)
+    queries = first[:, :q_rows].reshape(width, count)
+    keys = first[:, q_rows:].reshape(kv_width, count)
+    values = second[:, :k_rows].reshape(kv_width, count).astype(jnp.bfloat16)
+    turned_q = apply_rotation(queries, slot_positions, 1.0).astype(jnp.bfloat16)
+    turned_k = apply_rotation(keys, slot_positions, 1.0).astype(jnp.bfloat16)
     block_number = (slot_positions[0] // count).astype(jnp.bfloat16)
-    pack = jnp.concatenate([rotated_keys, value_matrix], axis=1)
-    pack = jnp.concatenate([pack, jnp.broadcast_to(block_number, (16, 2 * kv_width))], axis=0)
+    pack = jnp.concatenate(
+        [turned_k, values, jnp.broadcast_to(block_number, (16, count))], axis=0
+    )
     units_w = jnp.concatenate([w_gate, w_up, w_down], axis=0)
-    gathered, units_blocks = gather_blocks(
-        grid, 2, [pack, units_w], [GATHER_PART, ("shard",)]
-    )
-    block_numbers = gathered[:, count, 0].astype(jnp.int32)
+    pairs, units_blocks = gather_blocks(grid, 2, [pack, units_w], [GATHER_PART, ("shard",)])
+    block_numbers = pairs[:, 2 * kv_width, 0].astype(jnp.int32)
     key_places = (block_numbers[:, None] * count + jnp.arange(count)[None, :]).reshape(total_rows)
     query_places = jnp.tile(slot_positions, GROUP)
     bias = jnp.where(key_places[:, None] <= query_places[None, :], 0.0, -1e30).astype(jnp.float32)
-    by_head = gathered[:, :count].reshape(total_rows, 2, KEY_VALUE_HEADS, HEAD_WIDTH)
-    by_head = by_head.transpose(1, 2, 0, 3)
-    all_keys, all_values = by_head[0], by_head[1]
-    grouped_queries = to_groups(rotated_queries) * jnp.bfloat16(HEAD_WIDTH ** (-0.5))
-    mixed, norms = attend(grouped_queries, all_keys, all_values, bias)
-    mixed_low = from_groups(mixed)
-
-    middle = inputs + dot_last(mixed_low, out_w)
+    grouped_queries = (turned_q * jnp.bfloat16(HEAD_WIDTH ** (-0.5))).reshape(
+        QUERY_HEAD_COUNT, HEAD_WIDTH, count
+    )
+    mixed, norms = attend(grouped_queries, pairs, bias)
+    mixed_halves = mixed.reshape(shards, part, count)
+
+    branch = sum_halves(second_w, mixed_halves, dot_plain)[:, k_rows:].reshape(width, count)
+    middle = inputs + branch.T
     normed_two = rms_scale(middle, gain_two).astype(jnp.bfloat16)
     (normed_blocks,) = gather_blocks(grid, 3, [normed_two], [GATHER_PART])
     normed_all = normed_blocks.reshape(total_rows, width)
     units_full = units_blocks.transpose(1, 0, 2).reshape(3 * units, width)
-    gate_up = units_full[: 2 * units]
-    down_w = units_full[2 * units :]
-    gates_lifted = dot_last(normed_all, gate_up)
-    gates, lifted = gates_lifted[:, :units], gates_lifted[:, units:]
-    grad_hidden = dot_last(cot_all, down_w)
-    sigmoid = jax.nn.sigmoid(gates)
-    silu = gates * sigmoid
-    hidden = (silu * lifted).astype(jnp.bfloat16)
-    grad_gates = (grad_hidden * lifted * sigmoid * (1.0 + gates * (1.0 - sigmoid))).astype(
-        jnp.bfloat16
-    )
-    grad_lifted = (grad_hidden * silu).astype(jnp.bfloat16)
-    grad_both = jnp.concatenate([grad_gates, grad_lifted], axis=1)
-    grad_norm_part = dot_plain(grad_both, gate_up).astype(jnp.bfloat16)
-    unit_part = dot_plain(hidden, down_w).astype(jnp.bfloat16)
+    grad_norm_part, unit_part, grad_units = feed_forward(normed_all, cot_all, units_full)
     (grad_normed_two,) = scatter_sums(
         grid, 4, [grad_norm_part.reshape(devices, count, width)], [SCATTER_PART]
     )
+    unit_part, grad_normed_two = lax.optimization_barrier((unit_part, grad_normed_two))
     unit_out = lax.psum_scatter(
         unit_part, ("context", "tensor"), scatter_dimension=0, tiled=True
     ).astype(jnp.float32)
@@ -585,57 +649,77 @@
     grad_middle_norm, grad_gain_two = pull_two(grad_normed_two)
     grad_middle = incoming + grad_middle_norm
     grad_branch = grad_middle.astype(jnp.bfloat16)
-    mixed_gradient = dot_plain(grad_branch, out_w).astype(jnp.bfloat16)
+    blank_k = jnp.zeros((devices, k_rows, count), jnp.bfloat16)
+    blank_q = jnp.zeros((devices, q_rows, count), jnp.bfloat16)
+    grad_out_rows = jnp.concatenate(
+        [blank_k, grad_branch.T.reshape(devices, q_rows, count)], axis=1
+    ).reshape(flat, count)
+    mixed_gradient = jnp.concatenate(
+        [dot_first(second_w[at], grad_out_rows) for at in range(shards)], axis=0
+    ).astype(jnp.bfloat16)
     query_gradient, grad_keys, grad_values = attend_back(
-        grouped_queries, all_keys, all_values, bias, norms, to_groups(mixed_gradient)
-    )
-    key_terms = jnp.stack([grad_keys, grad_values]).transpose(2, 0, 1, 3)
-    key_terms = key_terms.reshape(devices, count, 2 * kv_width)
-    grad_gate_up = jnp.dot(grad_both.T, normed_all, preferred_element_type=jnp.float32)
-    grad_down = jnp.dot(hidden.T, cot_all, preferred_element_type=jnp.float32)
-    grad_units = jnp.concatenate([grad_gate_up, grad_down], axis=0).astype(jnp.bfloat16)
-    grad_units = grad_units.reshape(3 * units, shards, part).transpose(1, 0, 2)
-    summed, unit_sums = scatter_sums(
-        grid, 5, [key_terms, grad_units], [SCATTER_PART, ("shard",)]
-    )
-    grad_q = apply_rotation(
-        from_groups(query_gradient), slot_positions, QUERY_HEAD_COUNT, -1.0
-    ).astype(jnp.bfloat16)
-    key_gradient = apply_rotation(
-        summed[:, :kv_width], slot_positions, KEY_VALUE_HEADS, -1.0
-    ).astype(jnp.bfloat16)
-    grad_v = summed[:, kv_width:].astype(jnp.bfloat16)
-    grad_normed_one = (
-        dot_plain(grad_q, query_w) + dot_plain(key_gradient, key_w) + dot_plain(grad_v, value_w)
+        grouped_queries, pairs, bias, norms, mixed_gradient.reshape(grouped_queries.shape)
+    )
+    grad_units = grad_units.astype(jnp.bfloat16).reshape(3 * units, shards, part)
+    key_sum, value_sum, unit_sums = scatter_sums(
+        grid,
+        5,
+        [grad_keys, grad_values, grad_units.transpose(1, 0, 2)],
+        [SCATTER_PART, SCATTER_PART, ("shard",)],
+    )
+    grad_q = apply_rotation(query_gradient.reshape(width, count), slot_positions, -1.0)
+    grad_k = apply_rotation(key_sum, slot_positions, -1.0)
+    first_rows = jnp.concatenate(
+        [
+            grad_q.astype(jnp.bfloat16).reshape(devices, q_rows, count),
+            grad_k.astype(jnp.bfloat16).reshape(devices, k_rows, count),
+        ],
+        axis=1,
+    ).reshape(flat, count)
+    value_rows = jnp.concatenate(
+        [value_sum.astype(jnp.bfloat16).reshape(devices, k_rows, count), blank_q], axis=1
+    ).reshape(flat, count)
+    grad_normed_one = jnp.concatenate(
+        [
+            dot_first(first_rows, first_w[at]) + dot_first(value_rows, second_w[at])
+            for at in range(shards)
+        ],
+        axis=1,
     )
     unused_one, pull_one = jax.vjp(rms_scale, inputs, gain_one)
     grad_inputs_norm, grad_gain_one = pull_one(grad_normed_one)
     grad_tokens = (grad_middle + grad_inputs_norm).astype(jnp.bfloat16)[None]
-
-    def by_device(left, right):
-        grad = jnp.dot(left.T, right, preferred_element_type=jnp.float32).astype(jnp.bfloat16)
-        return grad.reshape(devices, grad.shape[0] // devices, shards, part)
-
-    grads = jnp.concatenate(
+    first_grads = jnp.stack(
+        [dot_plain(first_rows, half).astype(jnp.bfloat16) for half in normed_halves]
+    )
+    second_grads = jnp.stack(
         [
-            by_device(grad_q, normed_one),
-            by_device(key_gradient, normed_one),
-            by_device(grad_v, normed_one),
-            by_device(grad_branch, mixed_low),
-        ],
-        axis=1,
-    )
-    grads = grads.transpose(2, 0, 1, 3).reshape(shards * devices, packed.shape[0], part)
+            (
+                dot_plain(value_rows, normed_halves[at])
+                + dot_last(grad_out_rows, mixed_halves[at])
+            ).astype(jnp.bfloat16)
+            for at in range(shards)
+        ]
+    )
     gains = jnp.zeros((8, width), jnp.float32).at[0].set(grad_gain_one).at[1].set(grad_gain_two)
-    sums, gain_sums = scatter_sums(grid, 6, [grads], [SCATTER_ALL], gains)
+    first_sums, second_sums, gain_sums = scatter_sums(
+        grid,
+        6,
+        [
+            first_grads.reshape(shards * devices, both, part),
+            second_grads.reshape(shards * devices, both, part),
+        ],
+        SCATTER_ALL,
+        gains,
+    )
     return (
         output,
         grad_tokens,
         gain_sums[0],
-        sums[:q_end],
-        sums[q_end:k_end],
-        sums[k_end:v_end],
-        sums[v_end:],
+        first_sums[:q_rows],
+        first_sums[q_rows:],
+        second_sums[:k_rows],
+        second_sums[k_rows:],
         gain_sums[1],
         unit_sums[:units],
         unit_sums[units : 2 * units],

time: 549 us -> 404 us (0.74); the launches traced: 542 us -> 403 us
  local copies, waits for them, and re-layouts: 150 us -> 43.8 us
  matrix products: 43.6 us -> 17.6 us
  Pallas kernels: 292 us -> 307 us
  waiting for transfers between devices: 14.4 us -> 0.06 us
    reshape x19 -> x6, local copies, waits for them, and re-layouts: 73.9 us -> 5.92 us  [the longest x1 4.09 us: body(): units_full = units_blocks.transpose(1, 0, 2).reshape(3 * units, width)]
    slice x14 -> x9, local copies, waits for them, and re-layouts: 29.7 us -> 6.58 us  [the longest x1 3.2 us: sum_halves(): total = total + dot(weights[at], halves[at])]
    pallas_call x2 -> x3, Pallas kernels: 28.6 us -> 44.6 us  [the longest x1 16.4 us: attend_back(): pl.pallas_call(attend_back_kernel, grid=(KEY_VALUE_HEADS,), in_specs=[gro...]
    reduce_scatter x1, waiting for transfers between devices: 13.7 us -> 0.01 us  [body(): lax.psum_scatter(unit_part, ('context', 'tensor'), scatter_dimension=0, t...]
    dot_general x6, matrix products: 16.4 us -> 3.16 us  [dot_last(): lax.dot_general(left, right, (((1,), (1,)), ((), ())), preferred_element_...]
    dot_general x6, matrix products: 15.3 us -> 4.36 us  [dot_plain(): lax.dot_general(left, right, (((1,), (0,)), ((), ())), preferred_element_...]
    convert_element_type x4, local copies, waits for them, and re-layouts: 13.4 us -> 3.15 us  [the longest x1 2.36 us: body(): grad_units.astype(jnp.bfloat16).reshape(3 * units, shards, part)]
    dot_general x3 -> x0, local copies, waits for them, and re-layouts: 8.51 us -> none  [the longest x1 6.42 us: body(): jnp.dot(grad_both.T, normed_all, preferred_element_type=jnp.float32)]
  transfers between devices with their start and end apart: 2 -> 2, of which waited for: 1 -> 0; matrix products, arithmetic and copies ran while one was open for 23% -> 17% of each run, Pallas kernels for 36% -> 60%
where the time goes in v2:
time: 404 us; the launch traced here: 403 us
  Pallas kernels  307 us (76%)
  local copies, waits for them, and re-layouts  43.8 us (11%)
  other arithmetic  18.3 us (5%)
  matrix products  17.6 us (4%)
  between operations  16.2 us (4%)
    pallas_call x3, Pallas kernels, scatter_sums(): pl.pallas_call(functools.partial(scatter_kernel, grid, plans, gains is no...  135 us
    pallas_call x3, Pallas kernels, gather_blocks(): pl.pallas_call(functools.partial(gather_kernel, grid, plans), out_shape=[...  127 us
    pallas_call x1, Pallas kernels, attend_back(): pl.pallas_call(attend_back_kernel, grid=(KEY_VALUE_HEADS,), in_specs=[gro...  16.4 us
    pallas_call x1, Pallas kernels, feed_forward(): pl.pallas_call(functools.partial(units_kernel, units), grid=(total // row...  16.4 us
    unnamed x78, local copies, waits for them, and re-layouts  12 us
    pallas_call x1, Pallas kernels, attend(): pl.pallas_call(attend_kernel, grid=(KEY_VALUE_HEADS,), in_specs=[group_sp...  11.7 us
    dot_general x6, matrix products, dot_first(): lax.dot_general(left, right, (((0,), (0,)), ((), ())), preferred_element_...  10.1 us
  transfers between devices with their start and end apart: 2, of which 0 were waited for; matrix products, arithmetic and copies ran while one was open for 17% of the time, Pallas kernels for 60%

profile of v2, /device:TPU:0, one launch (start us, length us, event | category | flops | bytes accessed | tf_op | source)
XLA Modules:
  0.0 402.7 jit_solution(3810677653685701000)
XLA Ops:
  7.2 1.8 copy.55
  10.4 1.1 copy.53
  11.5 1.6 pad_maximum_fusion.7.refs_0_
  13.1 1.5 pad_maximum_fusion.8.refs_1_
  14.6 46.9 %gather_blocks_1.1 = (bf16[32,80,480]{2,1,0:T(8,128)(2,1)}, bf16[32,80,480]{2,1,0:T(8,128)(2,1)}) custom-call(bf16[80,480]{1,0:T(8,128)(2,1)} %pad_maximum_fusion.7.refs_0_, bf16[80,480]{1,0:T(8,128)(2,1)} %pad_maximum_fusion.8.refs_1_), custom_call_target="tpu_custom_call" | custom-call | bytes 78643200 | tf_op jit(solution)/shard_map/gather_blocks_1/pallas_call | solution.py:185
  61.6 0.8 fusion.13
  62.5 3.2 fusion.47
  65.7 0.5 fusion.35
  66.2 0.6 convolution_add_fusion.4
  66.8 0.7 slice.174
  68.3 0.6 fusion.6
  69.4 0.8 pad_maximum_fusion.3.refs_1_
  70.3 0.8 maximum_maximum_fusion.refs_0_
  71.1 39.0 %gather_blocks_2.1 = (bf16[16,656,128]{2,1,0:T(8,128)(2,1)}, bf16[2,480,480]{2,1,0:T(8,128)(2,1)}) custom-call(bf16[656,128]{1,0:T(8,128)(2,1)} %maximum_maximum_fusion.refs_0_, bf16[480,480]{1,0:T(8,128)(2,1)} %pad_maximum_fusion.3.refs_1_), custom_call_target="tpu_custom_call" | custom-call | bytes 57737216 | tf_op jit(solution)/shard_map/gather_blocks_2/pallas_call | solution.py:185
  110.1 3.4 copy.56
  113.5 4.1 %reshape.322.weights = bf16[480,960]{1,0:T(8,128)(2,1)} reshape(bf16[480,2,480]{2,1,0:T(2,128)(2,1)} %copy.56) | data formatting | bytes 1843200 | tf_op jit(solution)/shard_map/reshape | solution.py:637
  118.2 1.8 compare_select_fusion.bias
  120.1 11.7 %attend.1 = (bf16[15,64,128]{2,1,0:T(8,128)(2,1)S(1)}, f32[5,1,384]{2,1,0:T(1,128)S(1)}) custom-call(bf16[15,64,128]{2,1,0:T(8,128)(2,1)S(1)} %maximum_multiply_fusion.queries, bf16[16,656,128]{2,1,0:T(8,128)(2,1)S(1)} %copy-done, bf16[16,656,128]{2,1,0:T(8,128)(2,1)S(1)} %copy-done, f32[2048,384]{1,0:T(8,128)} %compare_select_fusion.bias), custom_call_target="tpu_custom_call" | custom-call | tf_op jit(solution)/shard_map/attend/pallas_call | solution.py:434
  132.3 0.9 copy-done.15
  134.4 0.8 multiply_convert_fusion.refs_0_
  135.2 41.3 %gather_blocks_3.1 = bf16[16,128,960]{2,1,0:T(8,128)(2,1)} custom-call(bf16[128,960]{1,0:T(8,128)(2,1)} %multiply_convert_fusion.refs_0_), custom_call_target="tpu_custom_call" | custom-call | bytes 62914560 | tf_op jit(solution)/shard_map/gather_blocks_3/pallas_call | solution.py:185
  176.6 16.4 %feed_forward.1 = (bf16[2048,960]{1,0:T(8,128)(2,1)}, bf16[2048,960]{1,0:T(8,128)(2,1)}, f32[480,960]{1,0:T(8,128)S(1)}) custom-call(bf16[2048,960]{1,0:T(8,128)(2,1)} %bitcast.122, bf16[2048,960]{1,0:T(8,128)(2,1)} %bitcast.131, bf16[480,960]{1,0:T(8,128)(2,1)S(1)} %copy-done.1), custom_call_target="tpu_custom_call" | custom-call | tf_op jit(solution)/shard_map/feed_forward/pallas_call | solution.py:512
  193.0 1.3 copy-done.2
  194.3 47.6 %scatter_sums_4.1 = f32[128,960]{1,0:T(8,128)S(1)} custom-call(bf16[16,128,960]{2,1,0:T(8,128)(2,1)} %bitcast.130), custom_call_target="tpu_custom_call" | custom-call | bytes 62914560 | tf_op jit(solution)/shard_map/scatter_sums_4/pallas_call | solution.py:358
  242.0 1.0 copy-done.12
  243.7 1.9 fusion.9
  245.5 1.9 fusion.10
  247.4 16.4 %attend_back.1 = (f32[15,64,128]{2,1,0:T(8,128)S(1)}, bf16[16,320,128]{2,1,0:T(8,128)(2,1)S(1)}, bf16[16,320,128]{2,1,0:T(8,128)(2,1)S(1)}) custom-call(bf16[15,64,128]{2,1,0:T(8,128)(2,1)S(1)} %maximum_multiply_fusion.queries, bf16[16,656,128]{2,1,0:T(8,128)(2,1)} %get-tuple-element.57.keys.values, bf16[16,656,128]{2,1,0:T(8,128)(2,1)} %get-tuple-element.57.keys.values, ...), custom_call_target="tpu_custom_call" | custom-call | tf_op jit(solution)/shard_map/attend_back/pallas_call | solution.py:457
  263.9 1.1 copy-done.4
  264.9 1.2 copy-done.6
  266.2 0.7 convert_element_type.105
  266.9 0.8 concatenate.54
  267.7 1.2 convert_element_type.106
  268.9 2.4 copy.59
  271.3 1.5 copy.60
  272.8 33.8 %scatter_sums_5.1 = (f32[320,128]{1,0:T(8,128)S(1)}, f32[320,128]{1,0:T(8,128)S(1)}, f32[480,480]{1,0:T(8,128)S(1)}) custom-call(bf16[16,320,128]{2,1,0:T(8,128)(2,1)S(1)} %copy-done.5, bf16[16,320,128]{2,1,0:T(8,128)(2,1)} %copy-done.6, bf16[2,480,480]{2,1,0:T(8,128)(2,1)S(1)} %bitcast.115), custom_call_target="tpu_custom_call" | custom-call | bytes 56688640 | tf_op jit(solution)/shard_map/scatter_sums_5/pallas_call | solution.py:358
  306.6 1.0 copy-done.7
  307.7 0.8 concatenate.59
  308.5 1.2 pad_maximum_fusion.4
  309.6 2.0 convolution_bitcast_fusion.4
  311.6 0.6 fusion.7
  312.2 0.8 copy.61
  313.0 2.0 convolution_bitcast_fusion.2
  315.0 1.9 fusion.8
  316.9 0.8 copy.62
  317.8 0.6 fusion.3
  318.4 0.5 fusion.2
  318.9 1.7 pad_maximum_fusion
  320.6 3.0 copy.63
  323.6 1.7 fusion.25
  326.4 0.5 fusion.30
  327.4 1.7 pad_maximum_fusion.1
  329.1 4.4 %copy.64 = bf16[2,1280,480]{2,1,0:T(8,128)(2,1)} copy(bf16[2,1280,480]{1,2,0:T(8,128)(2,1)} %pad_maximum_fusion.1) | data formatting | bytes 4915200 | tf_op jit(solution)/shard_map/stack | solution.py:695
  333.5 1.3 fusion.14
  335.2 53.4 %scatter_sums_6.1 = (f32[80,480]{1,0:T(8,128)S(1)}, f32[80,480]{1,0:T(8,128)S(1)}, f32[8,960]{1,0:T(8,128)S(1)}) custom-call(bf16[32,80,480]{2,1,0:T(8,128)(2,1)S(1)} %bitcast.114, bf16[32,80,480]{2,1,0:T(8,128)(2,1)} %bitcast.127, f32[8,960]{1,0:T(8,128)S(1)} %scatter.9.refs_2_), custom_call_target="tpu_custom_call" | custom-call | bytes 78643200 | tf_op jit(solution)/shard_map/scatter_sums_6/pallas_call | solution.py:358
  388.6 0.6 slice.162
  389.3 0.7 slice.161
  389.9 0.6 slice.163
  390.6 0.7 slice.164
  391.2 0.6 fusion.50
  391.8 1.0 fusion.49
  392.8 1.4 fusion.21
  394.2 0.8 copy.66
  395.0 0.8 copy.65
  (119 shorter events, 6.4 us)
Async XLA Ops:
  7.2 169.4 %all-gather.3.cloned.1.call-start = ((), (), s32[]{:S(2)}) async-start(), calls=%async_computation.2 | async-start | bytes 4456448 | tf_op jit(solution)/shard_map/all_gather | solution.py:594
  9.0 383.8 %reduce-scatter.2.cloned.1.call-start = ((), (), s32[]{:S(2)}) async-start(), calls=%async_computation.1 | async-start | bytes 4456448 | tf_op jit(solution)/shard_map/reduce_scatter | solution.py:643
  11.5 51.0 %copy-start.18 = (bf16[1,128,960]{2,1,0:T(8,128)(2,1)}, bf16[1,128,960]{2,1,0:T(8,128)(2,1)S(1)}, u32[]{:S(2)}) copy-start(bf16[1,128,960]{2,1,0:T(8,128)(2,1)S(1)} %copy.53) | copy-start | bytes 737284
  62.4 5.8 %copy-start.20 = (bf16[128,960]{1,0:T(8,128)(2,1)}, bf16[128,960]{1,0:T(8,128)(2,1)S(1)}, u32[]{:S(2)}) copy-start(bf16[128,960]{1,0:T(8,128)(2,1)S(1)} %fusion.13) | copy-start | bytes 737284
  65.7 2.0 copy-start.16
  65.7 2.6 copy-start.14
  66.2 1.4 copy-start.36
  68.2 0.9 copy-start.30
  68.2 1.2 copy-start.31
  68.2 1.2 copy-start.32
  68.2 1.2 copy-start.33
  110.1 7.5 %copy-start = (bf16[16,656,128]{2,1,0:T(8,128)(2,1)S(1)}, bf16[16,656,128]{2,1,0:T(8,128)(2,1)}, u32[]{:S(2)}) copy-start(bf16[16,656,128]{2,1,0:T(8,128)(2,1)} %get-tuple-element.57.keys.values) | copy-start | bytes 8060932
  120.0 11.7 %copy-start.17 = (bf16[16,80,480]{2,1,0:T(8,128)(2,1)S(1)}, bf16[16,80,480]{2,1,0:T(8,128)(2,1)}, u32[]{:S(2)}) copy-start(bf16[16,80,480]{2,1,0:T(8,128)(2,1)} %copy-done.16) | copy-start | bytes 3686404
  131.8 2.0 copy-start.9
  131.8 1.4 copy-start.15
  133.2 0.9 copy-start.19
  133.7 0.7 copy-start.34
  134.3 42.2 %copy-start.11 = (f32[128,960]{1,0:T(8,128)}, f32[128,960]{1,0:T(8,128)S(1)}, u32[]{:S(2)}) copy-start(f32[128,960]{1,0:T(8,128)S(1)} %get-tuple-element.113) | copy-start | bytes 1474564
  134.4 42.2 %copy-start.1 = (bf16[480,960]{1,0:T(8,128)(2,1)S(1)}, bf16[480,960]{1,0:T(8,128)(2,1)}, u32[]{:S(2)}) copy-start(bf16[480,960]{1,0:T(8,128)(2,1)} %reshape.322.weights) | copy-start | bytes 2764804
  193.0 1.3 copy-start.2
  242.0 1.0 copy-start.12
  242.0 1.2 copy-start.23
  263.9 1.1 copy-start.4
  264.9 1.2 copy-start.6
  266.1 1.7 copy-start.3
  268.9 3.9 copy-start.5
  306.6 1.0 copy-start.7
  307.7 3.9 copy-start.27
  313.0 4.7 %copy-start.21 = (bf16[128,960]{1,0:T(8,128)(2,1)S(1)}, bf16[128,960]{1,0:T(8,128)(2,1)}, u32[]{:S(2)}) copy-start(bf16[128,960]{1,0:T(8,128)(2,1)} %copy-done.20) | copy-start | bytes 737284
  323.6 1.7 copy-start.10
  323.6 1.7 copy-start.25
  325.3 1.0 copy-start.22
  325.3 1.1 copy-start.26
  329.1 4.4 %copy-start.35 = (f32[960]{0:T(1024)S(1)}, f32[960]{0:T(1024)}, u32[]{:S(2)}) copy-start(f32[960]{0:T(1024)} %param.18) | copy-start | bytes 11524
  335.2 56.6 %copy-start.8 = (f32[480,480]{1,0:T(8,128)S(1)}, f32[480,480]{1,0:T(8,128)}, u32[]{:S(2)}) copy-start(f32[480,480]{1,0:T(8,128)} %copy-done.7) | copy-start | bytes 2764804
  388.6 4.2 %copy-start.13 = (f32[128,960]{1,0:T(8,128)S(1)}, f32[128,960]{1,0:T(8,128)}, u32[]{:S(2)}) copy-start(f32[128,960]{1,0:T(8,128)} %copy-done.11) | copy-start | bytes 1474564
  388.6 4.2 %copy-start.24 = (bf16[1,128,960]{2,1,0:T(8,128)(2,1)S(1)}, bf16[1,128,960]{2,1,0:T(8,128)(2,1)}, u32[]{:S(2)}) copy-start(bf16[1,128,960]{2,1,0:T(8,128)(2,1)} %copy.55) | copy-start | bytes 737284
  388.6 4.2 %copy-start.28 = (f32[128,480]{1,0:T(8,128)S(1)}, f32[128,480]{1,0:T(8,128)}, u32[]{:S(2)}) copy-start(f32[128,480]{1,0:T(8,128)} %copy.61) | copy-start | bytes 737284
  388.6 4.2 %copy-start.29 = (f32[128,480]{1,0:T(8,128)S(1)}, f32[128,480]{1,0:T(8,128)}, u32[]{:S(2)}) copy-start(f32[128,480]{1,0:T(8,128)} %copy.62) | copy-start | bytes 737284
Sparse Core Ops, SparseCore 0:
  10.2 68.5 all-gather.2
  242.2 87.1 reduce-scatter.1

commit v3 on v2

--- a/solution.py
+++ b/solution.py
@@ -151,7 +151,11 @@
             choices = itertools.product(*[range(grid.size[axis]) for axis in stages])
             listed = [offsets for offsets in choices if arrival(offsets) == stage]
             everything += [(turn, at, offsets) for turn, offsets in enumerate(listed)]
-        for turn, at, offsets in sorted(everything):
+        if number > 2:
+            everything.sort(key=lambda item: (item[1], item[0]))
+        else:
+            everything.sort()
+        for turn, at, offsets in everything:
             stages = plans[at]
             sizes = [grid.size[axis] for axis in stages]
             block = targets[at].at[grid.slot(me, stages, offsets)]
@@ -476,10 +480,13 @@
     )(queries, pairs, pairs, bias, norms, gradient)
 
 
-def units_kernel(units, normed, cot, weights, grad_norm, unit_out, grads):
+def units_kernel(units, *refs):
+    *pieces, cot, weights, grad_norm, unit_out, grads = refs
+    blocks = pieces[0].shape[0]
     gate_w, up_w = weights[:units], weights[units : 2 * units]
     down_w = weights[2 * units :]
-    rows, incoming = normed[...], cot[...]
+    rows = jnp.concatenate([piece[at] for at in range(blocks) for piece in pieces], axis=0)
+    incoming = cot[...]
     gates, lifted = dot_last(rows, gate_w), dot_last(rows, up_w)
     grad_hidden = dot_last(incoming, down_w)
     sigmoid = jax.nn.sigmoid(gates)
@@ -503,25 +510,27 @@
     grads[2 * units :] += dot_first(hidden, incoming)
 
 
-def feed_forward(normed, cot, weights):
-    total, width = normed.shape
-    rows = 256
+def feed_forward(pieces, cot, weights):
+    total, width = cot.shape
+    blocks, height = 2, pieces[0].shape[1]
+    rows = blocks * height * len(pieces)
+    by_blocks = pl.BlockSpec((blocks, height, width), lambda step: (step, 0, 0))
     units = weights.shape[0] // 3
     by_rows = pl.BlockSpec((rows, width), lambda step: (step, 0))
     whole = pl.BlockSpec(weights.shape, lambda step: (0, 0))
     return pl.pallas_call(
         functools.partial(units_kernel, units),
         grid=(total // rows,),
-        in_specs=[by_rows, by_rows, whole],
+        in_specs=[by_blocks] * len(pieces) + [by_rows, whole],
         out_specs=[by_rows, by_rows, whole],
         out_shape=[
-            jax.ShapeDtypeStruct(normed.shape, jnp.bfloat16),
-            jax.ShapeDtypeStruct(normed.shape, jnp.bfloat16),
+            jax.ShapeDtypeStruct(cot.shape, jnp.bfloat16),
+            jax.ShapeDtypeStruct(cot.shape, jnp.bfloat16),
             jax.ShapeDtypeStruct(weights.shape, jnp.float32),
         ],
         compiler_params=pltpu.CompilerParams(vmem_limit_bytes=VMEM_LIMIT),
         name="feed_forward",
-    )(normed, cot, weights)
+    )(*pieces, cot, weights)
 
 
 def rms_scale(value_matrix, gain):
@@ -548,6 +557,7 @@
     ).reshape(features.shape)
 
 
+PIECES = 4
 GATHER_PART = ("hi", "lo", "tensor")
 GATHER_ALL = [("hi", "lo", "shard", "tensor"), ("hi", "shard", "lo", "tensor")]
 SCATTER_PART = ("tensor", "lo", "hi")
@@ -591,7 +601,6 @@
             total = total + dot(weights[at], halves[at])
         return total.reshape(devices, both, count)
 
-    cot_all = lax.all_gather(cotangent[0], ("context", "tensor"), axis=0, tiled=True)
     first_blocks, second_blocks = gather_blocks(
         grid,
         1,
@@ -601,6 +610,8 @@
         ],
         GATHER_ALL,
     )
+    first_blocks, own_cot = lax.optimization_barrier((first_blocks, cotangent[0]))
+    cot_all = lax.all_gather(own_cot, ("context", "tensor"), axis=0, tiled=True)
     first_w = first_blocks.reshape(shards, flat, part)
     second_w = second_blocks.reshape(shards, flat, part)
 
@@ -632,10 +643,11 @@
     branch = sum_halves(second_w, mixed_halves, dot_plain)[:, k_rows:].reshape(width, count)
     middle = inputs + branch.T
     normed_two = rms_scale(middle, gain_two).astype(jnp.bfloat16)
-    (normed_blocks,) = gather_blocks(grid, 3, [normed_two], [GATHER_PART])
-    normed_all = normed_blocks.reshape(total_rows, width)
+    height = count // PIECES
+    pieces = [normed_two[at * height : (at + 1) * height] for at in range(PIECES)]
+    normed_pieces = gather_blocks(grid, 3, pieces, [GATHER_PART] * PIECES)
     units_full = units_blocks.transpose(1, 0, 2).reshape(3 * units, width)
-    grad_norm_part, unit_part, grad_units = feed_forward(normed_all, cot_all, units_full)
+    grad_norm_part, unit_part, grad_units = feed_forward(normed_pieces, cot_all, units_full)
     (grad_normed_two,) = scatter_sums(
         grid, 4, [grad_norm_part.reshape(devices, count, width)], [SCATTER_PART]
     )

time: 404 us -> 388 us (0.960)
  Pallas kernels: 307 us -> 291 us
    pallas_call x3, Pallas kernels: 127 us -> 117 us  [gather_blocks(): pl.pallas_call(functools.partial(gather_kernel, grid, plans), out_shape=[...]
    pallas_call x3, Pallas kernels: 135 us -> 128 us  [scatter_sums(): pl.pallas_call(functools.partial(scatter_kernel, grid, plans, gains is no...]
    unnamed x78 -> x82, local copies, waits for them, and re-layouts: 12 us -> 14.2 us
  transfers between devices with their start and end apart: 2 -> 2, of which waited for: 0 -> 0; matrix products, arithmetic and copies ran while one was open for 17% -> 17% of each run, Pallas kernels for 60% -> 51%
where the time goes in v3:
time: 388 us; the launch traced here: 387 us
  Pallas kernels  291 us (75%)
  local copies, waits for them, and re-layouts  46 us (12%)
  matrix products  18.9 us (5%)
  between operations  16.3 us (4%)
  other arithmetic  15.4 us (4%)
    pallas_call x3, Pallas kernels, scatter_sums(): pl.pallas_call(functools.partial(scatter_kernel, grid, plans, gains is no...  128 us
    pallas_call x3, Pallas kernels, gather_blocks(): pl.pallas_call(functools.partial(gather_kernel, grid, plans), out_shape=[...  117 us
    pallas_call x1, Pallas kernels, feed_forward(): pl.pallas_call(functools.partial(units_kernel, units), grid=(total // row...  17.2 us
    pallas_call x1, Pallas kernels, attend_back(): pl.pallas_call(attend_back_kernel, grid=(KEY_VALUE_HEADS,), in_specs=[gro...  16.3 us
    unnamed x82, local copies, waits for them, and re-layouts  14.2 us
    pallas_call x1, Pallas kernels, attend(): pl.pallas_call(attend_kernel, grid=(KEY_VALUE_HEADS,), in_specs=[group_sp...  11.7 us
    dot_general x6, matrix products, dot_first(): lax.dot_general(left, right, (((0,), (0,)), ((), ())), preferred_element_...  11.4 us
  transfers between devices with their start and end apart: 2, of which 0 were waited for; matrix products, arithmetic and copies ran while one was open for 17% of the time, Pallas kernels for 51%

profile of v3, /device:TPU:0, one launch (start us, length us, event | category | flops | bytes accessed | tf_op | source)
XLA Modules:
  0.0 387.3 jit_solution(14616924099280148524)
XLA Ops:
  7.2 1.8 copy.52
  9.0 1.6 pad_maximum_fusion.7
  10.6 35.8 %gather_blocks_1.1 = (bf16[32,80,480]{2,1,0:T(8,128)(2,1)}, bf16[32,80,480]{2,1,0:T(8,128)(2,1)}) custom-call(bf16[80,480]{1,0:T(8,128)(2,1)} %get-tuple-element.152.refs_0_, bf16[80,480]{1,0:T(8,128)(2,1)} %get-tuple-element.153.refs_1_), custom_call_target="tpu_custom_call" | custom-call | bytes 78643200 | tf_op jit(solution)/shard_map/gather_blocks_1/pallas_call | solution.py:189
  47.8 1.1 copy.51
  49.6 0.5 copy-done.33
  50.1 0.8 fusion.13
  50.9 2.0 fusion.48
  53.4 0.6 convolution_add_fusion.4
  54.0 0.9 slice.187
  55.0 1.8 reshape_reshape.6
  57.1 0.5 fusion.33
  58.1 0.6 fusion.6
  59.1 0.9 pad_maximum_fusion.3.refs_1_
  59.9 0.8 maximum_maximum_fusion.refs_0_
  60.8 38.9 %gather_blocks_2.1 = (bf16[16,656,128]{2,1,0:T(8,128)(2,1)}, bf16[2,480,480]{2,1,0:T(8,128)(2,1)}) custom-call(bf16[656,128]{1,0:T(8,128)(2,1)} %maximum_maximum_fusion.refs_0_, bf16[480,480]{1,0:T(8,128)(2,1)} %pad_maximum_fusion.3.refs_1_), custom_call_target="tpu_custom_call" | custom-call | bytes 57737216 | tf_op jit(solution)/shard_map/gather_blocks_2/pallas_call | solution.py:189
  99.7 3.4 copy.54
  103.1 4.2 %reshape.318.refs_5_ = bf16[480,960]{1,0:T(8,128)(2,1)} reshape(bf16[480,2,480]{2,1,0:T(2,128)(2,1)} %copy.54) | data formatting | bytes 1843200 | tf_op jit(solution)/shard_map/reshape | solution.py:649
  108.0 1.9 compare_select_fusion.bias
  109.8 11.7 %attend.1 = (bf16[15,64,128]{2,1,0:T(8,128)(2,1)S(1)}, f32[5,1,384]{2,1,0:T(1,128)S(1)}) custom-call(bf16[15,64,128]{2,1,0:T(8,128)(2,1)S(1)} %maximum_multiply_fusion.queries, bf16[16,656,128]{2,1,0:T(8,128)(2,1)S(1)} %copy-done, bf16[16,656,128]{2,1,0:T(8,128)(2,1)S(1)} %copy-done, f32[2048,384]{1,0:T(8,128)} %compare_select_fusion.bias), custom_call_target="tpu_custom_call" | custom-call | tf_op jit(solution)/shard_map/attend/pallas_call | solution.py:438
  122.1 0.9 copy-done.13
  124.3 0.7 fusion.50
  125.0 42.5 %gather_blocks_3.1 = (bf16[16,32,960]{2,1,0:T(8,128)(2,1)}, bf16[16,32,960]{2,1,0:T(8,128)(2,1)}, bf16[16,32,960]{2,1,0:T(8,128)(2,1)}, bf16[16,32,960]{2,1,0:T(8,128)(2,1)}) custom-call(bf16[32,960]{1,0:T(8,128)(2,1)} %get-tuple-element.142.refs_0_, bf16[32,960]{1,0:T(8,128)(2,1)} %get-tuple-element.141.refs_1_, ...), custom_call_target="tpu_custom_call" | custom-call | bytes 62914560 | tf_op jit(solution)/shard_map/gather_blocks_3/pallas_call | solution.py:189
  167.6 1.2 copy-done.3
  168.8 1.2 copy-done.4
  170.0 1.2 copy-done.5
  171.2 17.2 %feed_forward.1 = (bf16[2048,960]{1,0:T(8,128)(2,1)}, bf16[2048,960]{1,0:T(8,128)(2,1)}, f32[480,960]{1,0:T(8,128)}) custom-call(bf16[16,32,960]{2,1,0:T(8,128)(2,1)S(1)} %copy-done.3, bf16[16,32,960]{2,1,0:T(8,128)(2,1)S(1)} %copy-done.4, bf16[16,32,960]{2,1,0:T(8,128)(2,1)S(1)} %copy-done.5, bf16[16,32,960]{2,1,0:T(8,128)(2,1)} %get-tuple-element.69.refs_3_, ...), custom_call_target="tpu_custom_call" | custom-call | tf_op jit(solution)/shard_map/feed_forward/pallas_call | solution.py:521
  188.5 40.1 %scatter_sums_4.1 = f32[128,960]{1,0:T(8,128)S(1)} custom-call(bf16[16,128,960]{2,1,0:T(8,128)(2,1)} %bitcast.126), custom_call_target="tpu_custom_call" | custom-call | bytes 62914560 | tf_op jit(solution)/shard_map/scatter_sums_4/pallas_call | solution.py:362
  228.8 0.7 copy-done.20
  230.0 1.9 fusion.9
  231.8 1.9 fusion.10
  233.7 16.3 %attend_back.1 = (f32[15,64,128]{2,1,0:T(8,128)S(1)}, bf16[16,320,128]{2,1,0:T(8,128)(2,1)S(1)}, bf16[16,320,128]{2,1,0:T(8,128)(2,1)S(1)}) custom-call(bf16[15,64,128]{2,1,0:T(8,128)(2,1)S(1)} %maximum_multiply_fusion.queries, bf16[16,656,128]{2,1,0:T(8,128)(2,1)} %get-tuple-element.64.keys.values, bf16[16,656,128]{2,1,0:T(8,128)(2,1)} %get-tuple-element.64.keys.values, ...), custom_call_target="tpu_custom_call" | custom-call | tf_op jit(solution)/shard_map/attend_back/pallas_call | solution.py:461
  250.1 1.1 copy-done.2
  251.3 0.8 concatenate.54
  252.1 1.7 convert_element_type.106
  253.8 1.4 copy.56
  255.2 1.5 copy.57
  256.6 38.5 %scatter_sums_5.1 = (f32[320,128]{1,0:T(8,128)S(1)}, f32[320,128]{1,0:T(8,128)S(1)}, f32[480,480]{1,0:T(8,128)S(1)}) custom-call(bf16[16,320,128]{2,1,0:T(8,128)(2,1)S(1)} %get-tuple-element.78.refs_0_, bf16[16,320,128]{2,1,0:T(8,128)(2,1)} %copy-done.2, bf16[2,480,480]{2,1,0:T(8,128)(2,1)S(1)} %bitcast.112), custom_call_target="tpu_custom_call" | custom-call | bytes 56688640 | tf_op jit(solution)/shard_map/scatter_sums_5/pallas_call | solution.py:362
  295.2 1.0 copy-done.6
  296.2 0.8 concatenate.59
  297.1 2.0 convolution_bitcast_fusion.4
  299.0 1.9 fusion.7
  300.9 0.9 copy.58
  301.8 2.0 convolution_bitcast_fusion.2
  303.8 1.9 fusion.8
  305.7 0.8 copy.59
  306.5 0.6 fusion.3
  307.1 0.5 fusion.2
  307.7 1.7 pad_maximum_fusion
  309.3 3.0 copy.60
  312.3 1.6 fusion.25
  315.0 0.5 fusion.30
  316.0 1.7 pad_maximum_fusion.1
  317.7 4.4 %copy.61 = bf16[2,1280,480]{2,1,0:T(8,128)(2,1)} copy(bf16[2,1280,480]{1,2,0:T(8,128)(2,1)} %pad_maximum_fusion.1) | data formatting | bytes 4915200 | tf_op jit(solution)/shard_map/stack | solution.py:707
  322.1 1.3 fusion.14
  323.8 49.3 %scatter_sums_6.1 = (f32[80,480]{1,0:T(8,128)S(1)}, f32[80,480]{1,0:T(8,128)S(1)}, f32[8,960]{1,0:T(8,128)S(1)}) custom-call(bf16[32,80,480]{2,1,0:T(8,128)(2,1)S(1)} %bitcast.111, bf16[32,80,480]{2,1,0:T(8,128)(2,1)} %bitcast.123, f32[8,960]{1,0:T(8,128)S(1)} %scatter.9.refs_2_), custom_call_target="tpu_custom_call" | custom-call | bytes 78643200 | tf_op jit(solution)/shard_map/scatter_sums_6/pallas_call | solution.py:362
  373.2 0.6 slice.178
  373.8 0.7 slice.177
  374.5 0.6 slice.179
  375.1 0.7 slice.180
  375.8 0.6 fusion.51
  376.4 1.0 fusion.49
  377.4 1.4 fusion.21
  378.8 0.8 copy.63
  379.6 0.8 copy.62
  (124 shorter events, 7.4 us)
Async XLA Ops:
  7.2 160.4 %all-gather.2.cloned.1.call-start = ((), (), s32[]{:S(2)}) async-start(), calls=%async_computation.1 | async-start | bytes 4456448 | tf_op jit(solution)/shard_map/all_gather | solution.py:614
  46.5 330.9 %reduce-scatter.2.cloned.1.call-start = ((), (), s32[]{:S(2)}) async-start(), calls=%async_computation.2 | async-start | bytes 4456448 | tf_op jit(solution)/shard_map/reduce_scatter | solution.py:655
  48.9 74.9 %copy-start.16 = (bf16[1,128,960]{2,1,0:T(8,128)(2,1)}, bf16[1,128,960]{2,1,0:T(8,128)(2,1)S(1)}, u32[]{:S(2)}) copy-start(bf16[1,128,960]{2,1,0:T(8,128)(2,1)S(1)} %copy.51) | copy-start | bytes 737284
  49.0 0.5 copy-start.37
  49.6 0.5 copy-start.33
  50.9 6.7 %copy-start.18 = (bf16[128,960]{1,0:T(8,128)(2,1)}, bf16[128,960]{1,0:T(8,128)(2,1)S(1)}, u32[]{:S(2)}) copy-start(bf16[128,960]{1,0:T(8,128)(2,1)S(1)} %fusion.13) | copy-start | bytes 737284
  53.4 1.5 copy-start.35
  53.4 3.5 copy-start.24
  57.0 1.1 copy-start.12
  57.1 1.7 copy-start.14
  57.1 2.0 copy-start.28
  57.1 2.0 copy-start.29
  57.1 2.0 copy-start.30
  59.9 47.8 %copy-start.27 = (f32[15,64,128]{2,1,0:T(8,128)S(1)}, f32[15,64,128]{2,1,0:T(8,128)}, u32[]{:S(2)}) copy-start(f32[15,64,128]{2,1,0:T(8,128)} %reshape_reshape.6) | copy-start | bytes 1474564
  99.7 7.6 %copy-start = (bf16[16,656,128]{2,1,0:T(8,128)(2,1)S(1)}, bf16[16,656,128]{2,1,0:T(8,128)(2,1)}, u32[]{:S(2)}) copy-start(bf16[16,656,128]{2,1,0:T(8,128)(2,1)} %get-tuple-element.64.keys.values) | copy-start | bytes 8060932
  99.7 8.2 %copy-start.36 = (s32[1,128]{1,0:T(1,128)S(1)}, s32[1,128]{1,0:T(1,128)}, u32[]{:S(2)}) copy-start(s32[1,128]{1,0:T(1,128)} %param.17) | copy-start | bytes 1540
  109.8 11.7 %copy-start.15 = (bf16[16,80,480]{2,1,0:T(8,128)(2,1)S(1)}, bf16[16,80,480]{2,1,0:T(8,128)(2,1)}, u32[]{:S(2)}) copy-start(bf16[16,80,480]{2,1,0:T(8,128)(2,1)} %copy-done.14) | copy-start | bytes 3686404
  121.5 2.0 copy-start.8
  121.6 1.4 copy-start.13
  123.5 0.7 copy-start.31
  123.5 44.0 %copy-start.1 = (bf16[480,960]{1,0:T(8,128)(2,1)S(1)}, bf16[480,960]{1,0:T(8,128)(2,1)}, u32[]{:S(2)}) copy-start(bf16[480,960]{1,0:T(8,128)(2,1)} %reshape.318.refs_5_) | copy-start | bytes 2764804
  124.0 104.8 %copy-start.10 = (f32[128,960]{1,0:T(8,128)}, f32[128,960]{1,0:T(8,128)S(1)}, u32[]{:S(2)}) copy-start(f32[128,960]{1,0:T(8,128)S(1)} %get-tuple-element.125) | copy-start | bytes 1474564
  167.5 1.2 copy-start.3
  168.8 1.2 copy-start.4
  170.0 1.2 copy-start.5
  228.6 1.0 copy-start.20
  250.0 1.1 copy-start.2
  295.2 1.0 copy-start.6
  301.8 4.7 %copy-start.19 = (bf16[128,960]{1,0:T(8,128)(2,1)S(1)}, bf16[128,960]{1,0:T(8,128)(2,1)}, u32[]{:S(2)}) copy-start(bf16[128,960]{1,0:T(8,128)(2,1)} %copy-done.18) | copy-start | bytes 737284
  312.3 1.7 copy-start.9
  312.3 1.7 copy-start.22
  314.0 1.0 copy-start.23
  317.7 4.4 %copy-start.17 = (bf16[1,128,960]{2,1,0:T(8,128)(2,1)S(1)}, bf16[1,128,960]{2,1,0:T(8,128)(2,1)}, u32[]{:S(2)}) copy-start(bf16[1,128,960]{2,1,0:T(8,128)(2,1)} %copy-done.16) | copy-start | bytes 737284
  317.7 4.4 %copy-start.32 = (f32[960]{0:T(1024)S(1)}, f32[960]{0:T(1024)}, u32[]{:S(2)}) copy-start(f32[960]{0:T(1024)} %param.18) | copy-start | bytes 11524
  317.7 4.4 %copy-start.34 = (f32[128]{0:T(128)S(1)}, f32[128]{0:T(128)}, u32[]{:S(2)}) copy-start(f32[128]{0:T(128)} %copy-done.33) | copy-start | bytes 1540
  323.8 52.0 %copy-start.38 = (f32[128]{0:T(128)S(1)}, f32[128]{0:T(128)}, u32[]{:S(2)}) copy-start(f32[128]{0:T(128)} %copy-done.37) | copy-start | bytes 1540
  323.8 52.6 %copy-start.7 = (f32[480,480]{1,0:T(8,128)S(1)}, f32[480,480]{1,0:T(8,128)}, u32[]{:S(2)}) copy-start(f32[480,480]{1,0:T(8,128)} %copy-done.6) | copy-start | bytes 2764804
  373.2 4.2 %copy-start.11 = (f32[128,960]{1,0:T(8,128)S(1)}, f32[128,960]{1,0:T(8,128)}, u32[]{:S(2)}) copy-start(f32[128,960]{1,0:T(8,128)} %copy-done.10) | copy-start | bytes 1474564
  373.2 4.2 %copy-start.21 = (bf16[1,128,960]{2,1,0:T(8,128)(2,1)S(1)}, bf16[1,128,960]{2,1,0:T(8,128)(2,1)}, u32[]{:S(2)}) copy-start(bf16[1,128,960]{2,1,0:T(8,128)(2,1)} %copy.52) | copy-start | bytes 737284
  373.2 4.2 %copy-start.25 = (f32[128,480]{1,0:T(8,128)S(1)}, f32[128,480]{1,0:T(8,128)}, u32[]{:S(2)}) copy-start(f32[128,480]{1,0:T(8,128)} %copy.58) | copy-start | bytes 737284
  373.2 4.2 %copy-start.26 = (f32[128,480]{1,0:T(8,128)S(1)}, f32[128,480]{1,0:T(8,128)}, u32[]{:S(2)}) copy-start(f32[128,480]{1,0:T(8,128)} %copy.59) | copy-start | bytes 737284
Sparse Core Ops, SparseCore 0:
  46.6 68.9 all-gather.1
  228.7 87.3 reduce-scatter.1
